TPU v7x, 32 devices: a whole 2x2x4 slice. The times are simulated.
32 devices in a mesh: section: 2 (over y), dp: 16 (over z, x, core).
Axes of the slice: x: 2, y: 2, z: 4, core: 2. Of those that a mesh axis runs over, the one named last changes fastest.
Arguments:
- tokens: bfloat16 [8192, 768], P('dp'), may hold values from -6 to 6
- images: bfloat16 [64, 576, 768], P('dp'), may hold values from -6 to 6
- segments: int32 [128, 64], P('dp'), may hold values from 0 to 2, never falling along the last dimension, each value on 1 to 40 neighbouring positions
- image_ids: int32 [128, 3], P('dp'), may hold values from 0 to 1
- cotangent: bfloat16 [2, 8192, 768], P('section', 'dp'), may hold values from -6 to 6
- norm_gain: float32 [2, 2, 768], P('section', None, 'dp'), may hold values from 0.5 to 1.5
- norm_bias: float32 [2, 2, 768], P('section', None, 'dp'), may hold values from -2 to 2
- qkv_weight: float32 [2, 768, 2304], P('section', 'dp'), may hold values from -0.21875 to 0.21875
- out_weight: float32 [2, 768, 768], P('section', 'dp'), may hold values from -0.625 to 0.625
- up_weight: float32 [2, 768, 3072], P('section', 'dp'), may hold values from -0.21875 to 0.21875
- down_weight: float32 [2, 3072, 768], P('section', 'dp'), may hold values from -0.109375 to 0.109375
- cross_gain: float32 [768], P(('section', 'dp')), may hold values from 0.5 to 1.5
- cross_bias: float32 [768], P(('section', 'dp')), may hold values from -2 to 2
- cross_query: float32 [768, 768], P(('section', 'dp')), may hold values from -0.21875 to 0.21875
- cross_kv: float32 [768, 1536], P(('section', 'dp')), may hold values from -0.21875 to 0.21875
- cross_out: float32 [768, 768], P(('section', 'dp')), may hold values from -1.75 to 1.75
Outputs:
- layer_out: bfloat16 [2, 8192, 768], P('section', 'dp')
- input_grad: float32 [2, 8192, 768], P('section', 'dp')
- image_grad: float32 [64, 576, 768], P('dp', None, 'section')
- norm_gain_grad: float32 [2, 2, 768], P('section', None, 'dp')
- norm_bias_grad: float32 [2, 2, 768], P('section', None, 'dp')
- qkv_weight_grad: float32 [2, 768, 2304], P('section', 'dp')
- out_weight_grad: float32 [2, 768, 768], P('section', 'dp')
- up_weight_grad: float32 [2, 768, 3072], P('section', 'dp')
- down_weight_grad: float32 [2, 3072, 768], P('section', 'dp')
- cross_gain_grad: float32 [768], P(('section', 'dp'))
- cross_bias_grad: float32 [768], P(('section', 'dp'))
- cross_query_grad: float32 [768, 768], P(('section', 'dp'))
- cross_kv_grad: float32 [768, 1536], P(('section', 'dp'))
- cross_out_grad: float32 [768, 768], P(('section', 'dp'))
Inputs may be any that keep to these rules, and one draw needn't show every extreme that they name: `segments`: within a row the caption numbers never fall; each of the 3 captions has 1 to 40 tokens. `image_ids`: the image of caption s of a row, counted among the 2 images of that row's block: rows k * 4 to (k + 1) * 4 - 1 use images k * 2 onward.
All inputs are finite; a program needn't handle non-finite values.
Results may differ from a plain program's by a relative error of at most 0.025.
Values may be sent and summed in bfloat16 or wider, within the bound.
No kernel may reach another device: no remote copies, remote signals or barrier semaphores. Data moves between devices by JAX's collectives and lax.ppermute only.
A program may use at most 256 MiB of HBM per device.

v0:
```python
from functools import partial

import jax
import jax.numpy as jnp
from jax import lax
from jax.sharding import PartitionSpec as P

HEADS = 12
HEAD_DIM = 64
PATCHES = 576
ROW_LEN = 64
SEGS = 3
MICRO = 2
IMG_MB = 2
ROWS_MB = 4


MASKED_SCORE = -1000000000.0
NORM_EPS = 1e-05


def shifted(shard, axis, by):
    length = lax.axis_size(axis)
    pairs = [(i, i + by) for i in range(length) if 0 <= i + by < length]
    return lax.ppermute(shard, axis, pairs)


def matmul(left, right):
    return jnp.dot(left, right, preferred_element_type=jnp.float32)


def matmul_tn(left, right):
    return lax.dot_general(
        left, right, (((0,), (0,)), ((), ())), preferred_element_type=jnp.float32
    )


def matmul_nt(left, right):
    return lax.dot_general(
        left, right, (((1,), (1,)), ((), ())), preferred_element_type=jnp.float32
    )


def layer_norm(residual, gain_vec, bias_vec):
    average = jnp.mean(residual, axis=-1, keepdims=True)
    centred = residual - average
    inv_scale = lax.rsqrt(jnp.mean(centred * centred, axis=-1, keepdims=True) + NORM_EPS)
    normed = centred * inv_scale
    return (normed * gain_vec.astype(jnp.float32) + bias_vec.astype(jnp.float32), normed, inv_scale)


def norm_grad(d_out, normed, inv_scale, gain_vec):
    gain_grad = jnp.sum(d_out * normed, axis=0)
    bias_grad = jnp.sum(d_out, axis=0)
    d_normed = d_out * gain_vec.astype(jnp.float32)
    d_input = inv_scale * (
        d_normed
        - jnp.mean(d_normed, axis=-1, keepdims=True)
        - normed * jnp.mean(d_normed * normed, axis=-1, keepdims=True)
    )
    return (d_input, gain_grad, bias_grad)


def attend_core(queries, key_heads, value_heads, allowed):
    scores = jnp.einsum(
        "bqhd,bkhd->bhqk", queries, key_heads, preferred_element_type=jnp.float32
    ) * HEAD_DIM ** (-0.5)
    scores = jnp.where(allowed, scores, MASKED_SCORE)
    row_max = jnp.max(scores, axis=-1, keepdims=True)
    exponent = jnp.exp(scores - row_max)
    row_total = jnp.sum(exponent, axis=-1, keepdims=True)
    attn_probs = (exponent / row_total).astype(jnp.bfloat16)
    mixed_heads = jnp.einsum(
        "bhqk,bkhd->bqhd", attn_probs, value_heads, preferred_element_type=jnp.float32
    )
    return (mixed_heads, row_max + jnp.log(row_total))


def attend_back(queries, key_heads, value_heads, allowed, log_total, d_mixed):
    score_scale = HEAD_DIM ** (-0.5)
    scores = (
        jnp.einsum("bqhd,bkhd->bhqk", queries, key_heads, preferred_element_type=jnp.float32)
        * score_scale
    )
    scores = jnp.where(allowed, scores, MASKED_SCORE)
    probs_full = jnp.exp(scores - log_total)
    attn_probs = probs_full.astype(jnp.bfloat16)
    mixed_heads = jnp.einsum(
        "bhqk,bkhd->bqhd", attn_probs, value_heads, preferred_element_type=jnp.float32
    )
    d_probs = jnp.einsum(
        "bqhd,bkhd->bhqk", d_mixed, value_heads, preferred_element_type=jnp.float32
    )
    d_scores = (
        probs_full * (d_probs - jnp.sum(probs_full * d_probs, axis=-1, keepdims=True))
    ).astype(jnp.bfloat16)
    d_query = (
        jnp.einsum("bhqk,bkhd->bqhd", d_scores, key_heads, preferred_element_type=jnp.float32)
        * score_scale
    )
    d_key = (
        jnp.einsum("bhqk,bqhd->bkhd", d_scores, queries, preferred_element_type=jnp.float32)
        * score_scale
    )
    d_value = jnp.einsum("bhqk,bqhd->bkhd", attn_probs, d_mixed, preferred_element_type=jnp.float32)
    return (d_query, d_key, d_value, mixed_heads)


def self_forward(residual, gain_vec, bias_vec, qkv_mat, out_mat, same_doc):
    row_count = same_doc.shape[0]
    hidden = layer_norm(residual, gain_vec, bias_vec)[0].astype(jnp.bfloat16)
    qkv_heads = (
        matmul(hidden, qkv_mat).astype(jnp.bfloat16).reshape(row_count, -1, 3, HEADS, HEAD_DIM)
    )
    mixed_heads, log_total = attend_core(
        qkv_heads[:, :, 0], qkv_heads[:, :, 1], qkv_heads[:, :, 2], same_doc[:, None]
    )
    mixed_flat = mixed_heads.reshape(residual.shape[0], -1).astype(jnp.bfloat16)
    return (residual + matmul(mixed_flat, out_mat), log_total)


def self_back(residual, d_residual, log_total, gain_vec, bias_vec, qkv_mat, out_mat, same_doc):
    row_count = same_doc.shape[0]
    token_count = residual.shape[0]
    normal_out, normed, inv_scale = layer_norm(residual, gain_vec, bias_vec)
    hidden = normal_out.astype(jnp.bfloat16)
    qkv_heads = (
        matmul(hidden, qkv_mat).astype(jnp.bfloat16).reshape(row_count, -1, 3, HEADS, HEAD_DIM)
    )
    d_branch = d_residual.astype(jnp.bfloat16)
    d_mixed = (
        matmul_nt(d_branch, out_mat).astype(jnp.bfloat16).reshape(row_count, -1, HEADS, HEAD_DIM)
    )
    d_query, d_key, d_value, mixed_heads = attend_back(
        qkv_heads[:, :, 0],
        qkv_heads[:, :, 1],
        qkv_heads[:, :, 2],
        same_doc[:, None],
        log_total,
        d_mixed,
    )
    out_grad = matmul_tn(mixed_heads.reshape(token_count, -1).astype(jnp.bfloat16), d_branch)
    d_qkv = (
        jnp.stack([d_query, d_key, d_value], axis=2).reshape(token_count, -1).astype(jnp.bfloat16)
    )
    qkv_grad = matmul_tn(hidden, d_qkv)
    d_input, gain_grad, bias_grad = norm_grad(
        matmul_nt(d_qkv, qkv_mat), normed, inv_scale, gain_vec
    )
    return (d_residual + d_input, gain_grad, bias_grad, qkv_grad, out_grad)


def cross_forward(residual, tied_image, image_block, cross_set):
    gain_vec, bias_vec, query_mat, kv_mat, out_mat = cross_set
    model_width = residual.shape[1]
    hidden = layer_norm(residual, gain_vec, bias_vec)[0].astype(jnp.bfloat16)
    queries = matmul(hidden, query_mat).astype(jnp.bfloat16).reshape(1, -1, HEADS, HEAD_DIM)
    image_kv = matmul(image_block, kv_mat).astype(jnp.bfloat16)
    key_heads = image_kv[:, :model_width].reshape(1, -1, HEADS, HEAD_DIM)
    value_heads = image_kv[:, model_width:].reshape(1, -1, HEADS, HEAD_DIM)
    mixed_heads, log_total = attend_core(queries, key_heads, value_heads, tied_image[None, None])
    mixed_flat = mixed_heads.reshape(residual.shape[0], -1).astype(jnp.bfloat16)
    return (residual + matmul(mixed_flat, out_mat), log_total)


def cross_back(residual, d_residual, log_total, tied_image, image_block, cross_set):
    gain_vec, bias_vec, query_mat, kv_mat, out_mat = cross_set
    model_width = residual.shape[1]
    token_count = residual.shape[0]
    patch_count = image_block.shape[0]
    normal_out, normed, inv_scale = layer_norm(residual, gain_vec, bias_vec)
    hidden = normal_out.astype(jnp.bfloat16)
    queries = matmul(hidden, query_mat).astype(jnp.bfloat16).reshape(1, -1, HEADS, HEAD_DIM)
    image_kv = matmul(image_block, kv_mat).astype(jnp.bfloat16)
    key_heads = image_kv[:, :model_width].reshape(1, -1, HEADS, HEAD_DIM)
    value_heads = image_kv[:, model_width:].reshape(1, -1, HEADS, HEAD_DIM)
    d_branch = d_residual.astype(jnp.bfloat16)
    d_mixed = matmul_nt(d_branch, out_mat).astype(jnp.bfloat16).reshape(1, -1, HEADS, HEAD_DIM)
    d_query, d_key, d_value, mixed_heads = attend_back(
        queries, key_heads, value_heads, tied_image[None, None], log_total, d_mixed
    )
    out_grad = matmul_tn(mixed_heads.reshape(token_count, -1).astype(jnp.bfloat16), d_branch)
    d_kv = jnp.concatenate(
        [d_key.reshape(patch_count, -1), d_value.reshape(patch_count, -1)], axis=1
    ).astype(jnp.bfloat16)
    kv_grad = matmul_tn(image_block, d_kv)
    d_image = matmul_nt(d_kv, kv_mat)
    d_query_flat = d_query.reshape(token_count, -1).astype(jnp.bfloat16)
    query_grad = matmul_tn(hidden, d_query_flat)
    d_input, gain_grad, bias_grad = norm_grad(
        matmul_nt(d_query_flat, query_mat), normed, inv_scale, gain_vec
    )
    return (d_residual + d_input, gain_grad, bias_grad, query_grad, kv_grad, out_grad, d_image)


def feed_forward(residual, gain_vec, bias_vec, up_mat, down_mat):
    hidden = layer_norm(residual, gain_vec, bias_vec)[0].astype(jnp.bfloat16)
    activated = jax.nn.gelu(matmul(hidden, up_mat), approximate=False).astype(jnp.bfloat16)
    return residual + matmul(activated, down_mat)


def feed_back(residual, d_residual, gain_vec, bias_vec, up_mat, down_mat):
    normal_out, normed, inv_scale = layer_norm(residual, gain_vec, bias_vec)
    hidden = normal_out.astype(jnp.bfloat16)
    upward = matmul(hidden, up_mat)
    activated, gelu_pull = jax.vjp(partial(jax.nn.gelu, approximate=False), upward)
    d_branch = d_residual.astype(jnp.bfloat16)
    down_grad = matmul_tn(activated.astype(jnp.bfloat16), d_branch)
    d_upward = gelu_pull(matmul_nt(d_branch, down_mat))[0].astype(jnp.bfloat16)
    up_grad = matmul_tn(hidden, d_upward)
    d_input, gain_grad, bias_grad = norm_grad(
        matmul_nt(d_upward, up_mat), normed, inv_scale, gain_vec
    )
    return (d_residual + d_input, gain_grad, bias_grad, up_grad, down_grad)


def store_block(buffer, new_value, slot_index, is_valid):
    previous = lax.dynamic_index_in_dim(buffer, slot_index, 0, keepdims=False)
    return lax.dynamic_update_index_in_dim(
        buffer, jnp.where(is_valid, new_value, previous), slot_index, 0
    )


def local(
    tokens,
    images,
    segments,
    image_ids,
    cotangent,
    norm_gain,
    norm_bias,
    qkv_weight,
    out_weight,
    up_weight,
    down_weight,
    cross_gain,
    cross_bias,
    cross_query,
    cross_kv,
    cross_out,
):
    section_index = lax.axis_index("section")
    multimodal = section_index == 1
    model_width = tokens.shape[1]
    block_tokens = ROWS_MB * ROW_LEN
    block_patches = IMG_MB * PATCHES
    layer_parts = (
        lax.all_gather(norm_gain.astype(jnp.bfloat16), "dp", axis=2, tiled=True),
        lax.all_gather(norm_bias.astype(jnp.bfloat16), "dp", axis=2, tiled=True),
        lax.all_gather(qkv_weight.astype(jnp.bfloat16), "dp", axis=1, tiled=True),
        lax.all_gather(out_weight.astype(jnp.bfloat16), "dp", axis=1, tiled=True),
        lax.all_gather(up_weight.astype(jnp.bfloat16), "dp", axis=1, tiled=True),
        lax.all_gather(down_weight.astype(jnp.bfloat16), "dp", axis=1, tiled=True),
    )
    layer_set = tuple((gathered_piece[0] for gathered_piece in layer_parts))
    cross_set = (
        lax.all_gather(cross_gain.astype(jnp.bfloat16), ("section", "dp"), axis=0, tiled=True),
        lax.all_gather(cross_bias.astype(jnp.bfloat16), ("section", "dp"), axis=0, tiled=True),
        lax.all_gather(cross_query.astype(jnp.bfloat16), ("section", "dp"), axis=0, tiled=True),
        lax.all_gather(cross_kv.astype(jnp.bfloat16), ("section", "dp"), axis=0, tiled=True),
        lax.all_gather(cross_out.astype(jnp.bfloat16), ("section", "dp"), axis=0, tiled=True),
    )

    def block_masks(micro_index):
        seg_rows = lax.dynamic_slice_in_dim(segments, micro_index * ROWS_MB, ROWS_MB, 0)
        id_rows = lax.dynamic_slice_in_dim(image_ids, micro_index * ROWS_MB, ROWS_MB, 0)
        position = lax.broadcasted_iota(jnp.int32, (ROW_LEN, ROW_LEN), 0)
        earlier = lax.broadcasted_iota(jnp.int32, (ROW_LEN, ROW_LEN), 1) <= position
        same_doc = (seg_rows[:, :, None] == seg_rows[:, None, :]) & earlier[None]
        slots = lax.broadcasted_iota(jnp.int32, (1, 1, SEGS), 2)
        token_image = jnp.sum(
            jnp.where(seg_rows[:, :, None] == slots, id_rows[:, None, :], 0), axis=-1
        ).reshape(-1)
        key_image = lax.broadcasted_iota(jnp.int32, (1, block_patches), 1) // PATCHES
        tied_image = token_image[:, None] == key_image
        image_block = lax.dynamic_slice_in_dim(images, micro_index * IMG_MB, IMG_MB, 0).reshape(
            block_patches, model_width
        )
        return (same_doc, tied_image, image_block)

    kept_states = jnp.zeros((MICRO, 3, block_tokens, model_width), jnp.float32)
    kept_self = jnp.zeros((MICRO, ROWS_MB, HEADS, ROW_LEN, 1), jnp.float32)
    kept_cross = jnp.zeros((MICRO, 1, HEADS, block_tokens, 1), jnp.float32)
    layer_outputs = jnp.zeros((MICRO, block_tokens, model_width), jnp.bfloat16)
    arriving = jnp.zeros((block_tokens, model_width), jnp.bfloat16)
    for tick_num in range(MICRO + 1):
        position_now = tick_num - section_index
        micro_index = jnp.clip(position_now, 0, MICRO - 1)
        is_valid = (position_now >= 0) & (position_now < MICRO)
        same_doc, tied_image, image_block = block_masks(micro_index)
        own_rows = lax.dynamic_slice_in_dim(
            tokens, micro_index * block_tokens, block_tokens, 0
        ).astype(jnp.float32)
        start_state = jnp.where(multimodal, arriving.astype(jnp.float32), own_rows)
        (
            forward_norm_gains,
            forward_norm_biases,
            forward_qkv_mat,
            forward_out_mat,
            forward_up_mat,
            forward_down_mat,
        ) = layer_set
        after_self, self_total = self_forward(
            start_state,
            forward_norm_gains[0],
            forward_norm_biases[0],
            forward_qkv_mat,
            forward_out_mat,
            same_doc,
        )

        def forward_with_cross(current, tied_now, image_now):
            return cross_forward(current, tied_now, image_now, cross_set)

        def forward_without_cross(current, tied_now, image_now):
            return (current, jnp.zeros((1, HEADS, current.shape[0], 1), jnp.float32))

        after_cross, cross_total = lax.cond(
            multimodal,
            forward_with_cross,
            forward_without_cross,
            after_self,
            tied_image,
            image_block,
        )
        final_state = feed_forward(
            after_cross,
            forward_norm_gains[1],
            forward_norm_biases[1],
            forward_up_mat,
            forward_down_mat,
        )
        final_state, after_self, after_cross, self_total, cross_total = (
            final_state,
            after_self,
            after_cross,
            self_total,
            cross_total,
        )
        kept_states = store_block(
            kept_states, jnp.stack([start_state, after_self, after_cross]), micro_index, is_valid
        )
        kept_self = store_block(kept_self, self_total, micro_index, is_valid)
        kept_cross = store_block(kept_cross, cross_total, micro_index, is_valid)
        leaving = final_state.astype(jnp.bfloat16)
        layer_outputs = store_block(layer_outputs, leaving, micro_index, is_valid)
        if tick_num < MICRO:
            arriving = shifted(leaving, "section", 1)
    layer_totals = tuple((jnp.zeros(weight_part.shape, jnp.float32) for weight_part in layer_set))
    cross_totals = tuple((jnp.zeros(weight_part.shape, jnp.float32) for weight_part in cross_set))
    input_grads = jnp.zeros((MICRO, block_tokens, model_width), jnp.float32)
    image_grads = jnp.zeros((MICRO, block_patches, model_width), jnp.float32)
    returning = jnp.zeros((block_tokens, model_width), jnp.bfloat16)
    for tick_num in range(MICRO + 1):
        position_now = tick_num - 1 + section_index
        micro_index = jnp.clip(position_now, 0, MICRO - 1)
        is_valid = (position_now >= 0) & (position_now < MICRO)
        same_doc, tied_image, image_block = block_masks(micro_index)
        own_grad = lax.dynamic_slice_in_dim(
            cotangent[0], micro_index * block_tokens, block_tokens, 0
        ).astype(jnp.float32)
        d_state = own_grad + jnp.where(multimodal, 0.0, returning.astype(jnp.float32))
        states = lax.dynamic_index_in_dim(kept_states, micro_index, 0, keepdims=False)
        self_total = lax.dynamic_index_in_dim(kept_self, micro_index, 0, keepdims=False)
        cross_total = lax.dynamic_index_in_dim(kept_cross, micro_index, 0, keepdims=False)
        backward_d_state = d_state
        norm_gains, norm_biases, qkv_mat, out_mat, up_mat, down_mat = layer_set
        backward_d_state, ffn_gain, ffn_bias, up_grad, down_grad = feed_back(
            states[2], backward_d_state, norm_gains[1], norm_biases[1], up_mat, down_mat
        )

        def backward_with_cross(current, grad_now, total_now, tied_now, image_now):
            return cross_back(current, grad_now, total_now, tied_now, image_now, cross_set)

        def backward_without_cross(current, grad_now, total_now, tied_now, image_now):
            zero_vec = jnp.zeros((model_width,), jnp.float32)
            zero_square = jnp.zeros((model_width, model_width), jnp.float32)
            return (
                grad_now,
                zero_vec,
                zero_vec,
                zero_square,
                jnp.zeros((model_width, 2 * model_width), jnp.float32),
                zero_square,
                jnp.zeros((image_now.shape[0], model_width), jnp.float32),
            )

        cross_results = lax.cond(
            multimodal,
            backward_with_cross,
            backward_without_cross,
            states[1],
            backward_d_state,
            cross_total,
            tied_image,
            image_block,
        )
        backward_d_state, attn_gain, attn_bias, qkv_grad, out_grad = self_back(
            states[0],
            cross_results[0],
            self_total,
            norm_gains[0],
            norm_biases[0],
            qkv_mat,
            out_mat,
            same_doc,
        )
        layer_terms = (
            jnp.stack([attn_gain, ffn_gain]),
            jnp.stack([attn_bias, ffn_bias]),
            qkv_grad,
            out_grad,
            up_grad,
            down_grad,
        )
        d_input, layer_terms, cross_terms, image_term = (
            backward_d_state,
            layer_terms,
            cross_results[1:6],
            cross_results[6],
        )
        layer_terms = tuple((jnp.where(is_valid, grad_term, 0.0) for grad_term in layer_terms))
        cross_terms = tuple((jnp.where(is_valid, grad_term, 0.0) for grad_term in cross_terms))
        input_grads = store_block(input_grads, d_input, micro_index, is_valid)
        image_grads = store_block(image_grads, image_term, micro_index, is_valid)
        layer_totals = tuple(
            (total_part + new_part for total_part, new_part in zip(layer_totals, layer_terms))
        )
        cross_totals = tuple(
            (total_part + new_part for total_part, new_part in zip(cross_totals, cross_terms))
        )
        if tick_num < MICRO:
            returning = shifted(d_input.astype(jnp.bfloat16), "section", -1)
    layer_shards = (
        lax.psum_scatter(layer_totals[0][None], "dp", scatter_dimension=2, tiled=True),
        lax.psum_scatter(layer_totals[1][None], "dp", scatter_dimension=2, tiled=True),
        lax.psum_scatter(layer_totals[2][None], "dp", scatter_dimension=1, tiled=True),
        lax.psum_scatter(layer_totals[3][None], "dp", scatter_dimension=1, tiled=True),
        lax.psum_scatter(layer_totals[4][None], "dp", scatter_dimension=1, tiled=True),
        lax.psum_scatter(layer_totals[5][None], "dp", scatter_dimension=1, tiled=True),
    )
    cross_shards = (
        lax.psum_scatter(cross_totals[0], ("section", "dp"), scatter_dimension=0, tiled=True),
        lax.psum_scatter(cross_totals[1], ("section", "dp"), scatter_dimension=0, tiled=True),
        lax.psum_scatter(cross_totals[2], ("section", "dp"), scatter_dimension=0, tiled=True),
        lax.psum_scatter(cross_totals[3], ("section", "dp"), scatter_dimension=0, tiled=True),
        lax.psum_scatter(cross_totals[4], ("section", "dp"), scatter_dimension=0, tiled=True),
    )
    image_shard = lax.psum_scatter(
        image_grads.reshape(MICRO * IMG_MB, PATCHES, model_width).astype(jnp.bfloat16),
        "section",
        scatter_dimension=2,
        tiled=True,
    ).astype(jnp.float32)
    return (
        layer_outputs.reshape(1, -1, model_width),
        input_grads.reshape(1, -1, model_width),
        image_shard,
        layer_shards[0],
        layer_shards[1],
        layer_shards[2],
        layer_shards[3],
        layer_shards[4],
        layer_shards[5],
        cross_shards[0],
        cross_shards[1],
        cross_shards[2],
        cross_shards[3],
        cross_shards[4],
    )


def solution(mesh):
    in_specs = (
        P("dp", None),
        P("dp", None, None),
        P("dp", None),
        P("dp", None),
        P("section", "dp", None),
        P("section", None, "dp"),
        P("section", None, "dp"),
        P("section", "dp", None),
        P("section", "dp", None),
        P("section", "dp", None),
        P("section", "dp", None),
        P(("section", "dp")),
        P(("section", "dp")),
        P(("section", "dp"), None),
        P(("section", "dp"), None),
        P(("section", "dp"), None),
    )
    out_specs = (
        P("section", "dp", None),
        P("section", "dp", None),
        P("dp", None, "section"),
        P("section", None, "dp"),
        P("section", None, "dp"),
        P("section", "dp", None),
        P("section", "dp", None),
        P("section", "dp", None),
        P("section", "dp", None),
        P(("section", "dp")),
        P(("section", "dp")),
        P(("section", "dp"), None),
        P(("section", "dp"), None),
        P(("section", "dp"), None),
    )
    return jax.shard_map(local, mesh=mesh, in_specs=in_specs, out_specs=out_specs, check_vma=False)
```

profile of v0, /device:TPU:0, one launch (start us, length us, event | category | flops | bytes accessed | tf_op | source)
XLA Modules:
  0.0 1839.8 jit_solution(14326149553855617320)
XLA Ops:
  19.1 42.4 %all-reduce.5 = (bf16[768]{0:T(1024)(128)(2,1)}, bf16[768]{0:T(1024)(128)(2,1)}) all-reduce(bf16[768]{0:T(1024)(128)(2,1)S(1)} %dynamic-update-slice, bf16[768]{0:T(1024)(128)(2,1)S(1)} %dynamic-update-slice.1), channel_id=1, replica_groups=mesh['section'=2,'dp'=16] {'section','dp'}, use_global_device_ids=true, to_apply=%add | all-reduce | flops 1536 | bytes 6144
  61.5 22.5 %all_gather.34 = bf16[1,2,768]{1,0,2:T(2,128)(2,1)S(1)} all-gather(bf16[1,2,48]{1,0,2:T(2,128)(2,1)S(1)} %copy.434), channel_id=1, replica_groups=mesh['section'=2,'dp'=16] {'dp'}, dimensions={2}, use_global_device_ids=true | all-gather | bytes 3264 | tf_op jit(solution)/shard_map/all_gather | solution.py:249
  84.0 18.8 %all_gather.33 = bf16[1,2,768]{1,0,2:T(2,128)(2,1)S(1)} all-gather(bf16[1,2,48]{1,0,2:T(2,128)(2,1)S(1)} %copy.433), channel_id=1, replica_groups=mesh['section'=2,'dp'=16] {'dp'}, dimensions={2}, use_global_device_ids=true | all-gather | bytes 3264 | tf_op jit(solution)/shard_map/all_gather | solution.py:248
  103.9 4.6 fusion.457
  108.5 4.6 fusion.458
  131.1 27.7 %all-gather.14.cloned.1.call-done = bf16[768,768]{1,0:T(8,128)(2,1)} async-done(((bf16[24,768]{1,0:T(8,128)(2,1)}), bf16[768,768]{1,0:T(8,128)(2,1)}) %all-gather.14.cloned.1.call-update) | async-done | bytes 1179664 | tf_op jit(solution)/shard_map/all_gather | solution.py:259
  158.8 56.3 %all-gather.16.cloned.1.call-done = bf16[768,768]{1,0:T(8,128)(2,1)} async-done(((bf16[24,768]{1,0:T(8,128)(2,1)}), bf16[768,768]{1,0:T(8,128)(2,1)}) %all-gather.16.cloned.1.call-update) | async-done | bytes 1179664 | tf_op jit(solution)/shard_map/all_gather | solution.py:261
  215.0 59.5 %all-gather.12.cloned.1.call-done = bf16[768,1536]{1,0:T(8,128)(2,1)} async-done(((bf16[24,1536]{1,0:T(8,128)(2,1)}), bf16[768,1536]{1,0:T(8,128)(2,1)}) %all-gather.12.cloned.1.call-update) | async-done | bytes 2359312 | tf_op jit(solution)/shard_map/all_gather | solution.py:260
  279.8 49.8 %all-gather.20.cloned.1.call-done = bf16[1,3072,768]{2,1,0:T(8,128)(2,1)} async-done(((bf16[1,192,768]{2,1,0:T(8,128)(2,1)}), bf16[1,3072,768]{2,1,0:T(8,128)(2,1)}) %all-gather.20.cloned.1.call-update) | async-done | bytes 4718608 | tf_op jit(solution)/shard_map/all_gather | solution.py:253
  329.5 54.7 %all-gather.18.cloned.1.call-done = bf16[1,768,3072]{2,1,0:T(8,128)(2,1)} async-done(((bf16[1,48,3072]{2,1,0:T(8,128)(2,1)}), bf16[1,768,3072]{2,1,0:T(8,128)(2,1)}) %all-gather.18.cloned.1.call-update) | async-done | bytes 4718608 | tf_op jit(solution)/shard_map/all_gather | solution.py:252
  384.3 13.1 bitcast_dynamic-update-slice_fusion.7
  401.9 7.7 collective-permute-done
  431.0 7.9 conditional.7
  441.5 14.1 bitcast_dynamic-update-slice_fusion.6
  455.6 33.2 %collective-permute-start.1 = (bf16[256,768]{1,0:T(8,128)(2,1)}, bf16[256,768]{1,0:T(8,128)(2,1)S(1)}, u32[]{:S(2)}, u32[]{:S(2)}) collective-permute-start(bf16[256,768]{1,0:T(8,128)(2,1)} %get-tuple-element.1117), channel_id=1, source_target_pairs={{0,16},{1,17},{2,18},{3,19},{4,20},{5,21},{6,22},{7,23},{8,24},{9,... | collective-permute-start | bytes 1179656 | tf_op jit(solution)/shard_map/ppermute | solution.py:25
  489.0 7.7 collective-permute-done.1
  507.2 4.5 reshape.1805
  529.6 8.2 conditional.8
  551.1 8.9 add_convert_fusion.17
  562.6 14.7 conditional.9
  587.3 4.6 reshape.1830
  600.6 5.4 copy.468
  606.0 4.6 convert_element_type.893
  624.4 86.3 %collective-permute-done.2 = bf16[256,768]{1,0:T(8,128)(2,1)S(1)} collective-permute-done((bf16[256,768]{1,0:T(8,128)(2,1)S(1)}, bf16[256,768]{1,0:T(8,128)(2,1)S(1)}, u32[]{:S(2)}, u32[]{:S(2)}) %collective-permute-start.2) | collective-permute-done | bytes 393248 | tf_op jit(solution)/shard_map/ppermute | solution.py:25
  710.7 9.4 add_convert_fusion.16
  724.3 14.6 conditional.10
  757.4 5.4 copy.484
  785.5 52.7 %collective-permute-done.3 = bf16[256,768]{1,0:T(8,128)(2,1)S(1)} collective-permute-done((bf16[256,768]{1,0:T(8,128)(2,1)S(1)}, bf16[256,768]{1,0:T(8,128)(2,1)S(1)}, u32[]{:S(2)}, u32[]{:S(2)}) %collective-permute-start.3) | collective-permute-done | bytes 393248 | tf_op jit(solution)/shard_map/ppermute | solution.py:25
  838.2 9.4 add_convert_fusion.15
  852.4 15.8 conditional.11
  893.4 5.5 multiply_reduce_fusion.22
  908.3 5.6 copy.543
  913.8 7.8 reshape.1824
  950.9 7.6 select_add_fusion
  964.8 6.1 add_bitcast_fusion.5
  978.0 6.2 add_bitcast_fusion.4
  985.3 9.7 fusion.234
  995.1 10.1 fusion.235
  1005.2 12.7 add_bitcast_fusion.3
  1023.6 13.2 fusion.409
  1038.5 94.5 %all-reduce.4 = (f32[768]{0:T(1024)S(1)}, f32[768]{0:T(1024)S(1)}) all-reduce(f32[768]{0:T(1024)S(1)} %select_add_fusion.4, f32[768]{0:T(1024)S(1)} %select_add_fusion.3), channel_id=9, replica_groups=mesh['section'=2,'dp'=16] {'section','dp'}, use_global_device_ids=true, to_apply=%region_115.116.clone | all-reduce | flops 1536 | bytes 12288
  1150.2 74.5 %reduce-scatter.25.cloned.1.call-done = f32[24,768]{1,0:T(8,128)} async-done(((f32[768,768]{1,0:T(8,128)}), f32[24,768]{1,0:T(8,128)}) %reduce-scatter.25.cloned.1.call-update) | async-done | bytes 73744 | tf_op jit(solution)/shard_map/reduce_scatter | solution.py:445
  1224.7 103.7 %reduce-scatter.29.cloned.1.call-done = f32[24,768]{1,0:T(8,128)} async-done(((f32[768,768]{1,0:T(8,128)}), f32[24,768]{1,0:T(8,128)}) %reduce-scatter.29.cloned.1.call-update) | async-done | bytes 73744 | tf_op jit(solution)/shard_map/reduce_scatter | solution.py:447
  1328.4 66.9 %reduce-scatter.19.cloned.1.call-done = f32[1,48,768]{2,1,0:T(8,128)} async-done(((f32[1,768,768]{2,1,0:T(8,128)}), f32[1,48,768]{2,1,0:T(8,128)}) %reduce-scatter.19.cloned.1.call-update) | async-done | bytes 147472 | tf_op jit(solution)/shard_map/reduce_scatter | solution.py:438
  1395.2 112.0 %reduce-scatter.27.cloned.1.call-done = f32[24,1536]{1,0:T(8,128)} async-done(((f32[768,1536]{1,0:T(8,128)}), f32[24,1536]{1,0:T(8,128)}) %reduce-scatter.27.cloned.1.call-update) | async-done | bytes 147472 | tf_op jit(solution)/shard_map/reduce_scatter | solution.py:446
  1507.2 94.1 %reduce-scatter.17.cloned.1.call-done = f32[1,48,2304]{2,1,0:T(8,128)} async-done(((f32[1,768,2304]{2,1,0:T(8,128)}), f32[1,48,2304]{2,1,0:T(8,128)}) %reduce-scatter.17.cloned.1.call-update) | async-done | bytes 442384 | tf_op jit(solution)/shard_map/reduce_scatter | solution.py:437
  1601.4 115.4 %reduce-scatter.21.cloned.1.call-done = f32[1,48,3072]{2,1,0:T(8,128)} async-done(((f32[1,768,3072]{2,1,0:T(8,128)}), f32[1,48,3072]{2,1,0:T(8,128)}) %reduce-scatter.21.cloned.1.call-update) | async-done | bytes 589840 | tf_op jit(solution)/shard_map/reduce_scatter | solution.py:439
  1716.8 116.2 %reduce-scatter.23.cloned.1.call-done = f32[1,192,768]{2,1,0:T(8,128)} async-done(((f32[1,3072,768]{2,1,0:T(8,128)}), f32[1,192,768]{2,1,0:T(8,128)}) %reduce-scatter.23.cloned.1.call-update) | async-done | bytes 589840 | tf_op jit(solution)/shard_map/reduce_scatter | solution.py:440
  (665 shorter events, 318.2 us)
Async XLA Ops:
  7.2 95.6 %copy-start.24 = (bf16[512,768]{1,0:T(8,128)(2,1)S(1)}, bf16[512,768]{1,0:T(8,128)(2,1)}, u32[]{:S(2)}) copy-start(bf16[512,768]{1,0:T(8,128)(2,1)} %param.28) | copy-start | bytes 2359300
  7.2 96.3 %copy-start.129 = (s32[8,64]{1,0:T(8,128)S(1)}, s32[8,64]{1,0:T(8,128)}, u32[]{:S(2)}) copy-start(s32[8,64]{1,0:T(8,128)} %param.30) | copy-start | bytes 6148
  7.3 106.9 %all-gather.8.cloned.1.call-start = ((), (), s32[]{:S(2)}) async-start(), calls=%async_computation.10 | async-start | bytes 3760128 | tf_op jit(solution)/shard_map/all_gather | solution.py:250
  9.1 119.2 %all-gather.10.cloned.1.call-start = ((), (), s32[]{:S(2)}) async-start(), calls=%async_computation.11 | async-start | bytes 1253376 | tf_op jit(solution)/shard_map/all_gather | solution.py:251
  10.8 148.0 %all-gather.14.cloned.1.call-start = ((), (), s32[]{:S(2)}) async-start(), calls=%async_computation.13 | async-start | bytes 1216512 | tf_op jit(solution)/shard_map/all_gather | solution.py:259
  12.3 202.7 %all-gather.16.cloned.1.call-start = ((), (), s32[]{:S(2)}) async-start(), calls=%async_computation.14 | async-start | bytes 1216512 | tf_op jit(solution)/shard_map/all_gather | solution.py:261
  13.9 260.6 %all-gather.12.cloned.1.call-start = ((), (), s32[]{:S(2)}) async-start(), calls=%async_computation.12 | async-start | bytes 2433024 | tf_op jit(solution)/shard_map/all_gather | solution.py:260
  15.6 314.0 %all-gather.20.cloned.1.call-start = ((), (), s32[]{:S(2)}) async-start(), calls=%async_computation.16 | async-start | bytes 5013504 | tf_op jit(solution)/shard_map/all_gather | solution.py:253
  17.4 366.8 %all-gather.18.cloned.1.call-start = ((), (), s32[]{:S(2)}) async-start(), calls=%async_computation.15 | async-start | bytes 5013504 | tf_op jit(solution)/shard_map/all_gather | solution.py:252
  18.3 1118.0 %reduce-scatter.33.cloned.1.call-start = ((), (), s32[]{:S(2)}) async-start(), calls=%async_computation.25 | async-start | bytes 417792
  108.5 392.0 %copy-start.107 = (f32[768]{0:T(1024)}, f32[768]{0:T(1024)S(1)}, u32[]{:S(2)}) copy-start(f32[768]{0:T(1024)S(1)} %get-tuple-element.1027) | copy-start | bytes 9220
  108.5 672.9 %copy-start.105 = (f32[768]{0:T(1024)}, f32[768]{0:T(1024)S(1)}, u32[]{:S(2)}) copy-start(f32[768]{0:T(1024)S(1)} %get-tuple-element.1026) | copy-start | bytes 9220
  113.2 387.3 %copy-start.102 = (f32[768]{0:T(1024)}, f32[768]{0:T(1024)S(1)}, u32[]{:S(2)}) copy-start(f32[768]{0:T(1024)S(1)} %get-tuple-element.1025) | copy-start | bytes 9220
  127.2 147.3 %copy-start.142 = (s32[1152]{0:T(1024)S(1)}, s32[1152]{0:T(1024)}, u32[]{:S(2)}) copy-start(s32[1152]{0:T(1024)} %add_select_fusion) | copy-start | bytes 13828
  127.2 147.4 %copy-start.126 = (bf16[768]{0:T(1024)(128)(2,1)S(1)}, bf16[768]{0:T(1024)(128)(2,1)}, u32[]{:S(2)}) copy-start(bf16[768]{0:T(1024)(128)(2,1)} %get-tuple-element.1030) | copy-start | bytes 4612
  127.2 147.4 %copy-start.127 = (bf16[768]{0:T(1024)(128)(2,1)S(1)}, bf16[768]{0:T(1024)(128)(2,1)}, u32[]{:S(2)}) copy-start(bf16[768]{0:T(1024)(128)(2,1)} %get-tuple-element.1031) | copy-start | bytes 4612
  127.2 147.4 %copy-start.128 = (s32[8,3]{0,1:T(4,128)S(1)}, s32[8,3]{0,1:T(4,128)}, u32[]{:S(2)}) copy-start(s32[8,3]{0,1:T(4,128)} %param.31) | copy-start | bytes 292
  127.2 147.4 %copy-start.141 = (s32[4,64]{1,0:T(4,128)S(1)}, s32[4,64]{1,0:T(4,128)}, u32[]{:S(2)}) copy-start(s32[4,64]{1,0:T(4,128)} %copy-done.140) | copy-start | bytes 3076
  397.4 12.2 collective-permute-start
  455.6 41.1 %collective-permute-start.1 = (bf16[256,768]{1,0:T(8,128)(2,1)}, bf16[256,768]{1,0:T(8,128)(2,1)S(1)}, u32[]{:S(2)}, u32[]{:S(2)}) collective-permute-start(bf16[256,768]{1,0:T(8,128)(2,1)} %get-tuple-element.1117), channel_id=1, source_target_pairs={{0,16},{1,17},{2,18},{3,19},{4,20},{5,21},{6,22},{7,23},{8,24},{9,... | collective-permute-start | bytes 1179656 | tf_op jit(solution)/shard_map/ppermute | solution.py:25
  616.3 94.4 %collective-permute-start.2 = (bf16[256,768]{1,0:T(8,128)(2,1)S(1)}, bf16[256,768]{1,0:T(8,128)(2,1)S(1)}, u32[]{:S(2)}, u32[]{:S(2)}) collective-permute-start(bf16[256,768]{1,0:T(8,128)(2,1)S(1)} %get-tuple-element.1034), channel_id=1, source_target_pairs={{16,0},{17,1},{18,2},{19,3},{20,4},{21,5},{22,6},{23,7},{24,8},{25... | collective-permute-start | bytes 1179656 | tf_op jit(solution)/shard_map/ppermute | solution.py:25
  617.8 105.2 %copy-start.159 = (f32[256]{0:T(256)}, f32[256]{0:T(256)S(1)}, u32[]{:S(2)}) copy-start(f32[256]{0:T(256)S(1)} %add_rsqrt_fusion.9) | copy-start | bytes 3076
  618.7 92.0 %slice-start.6 = ((s8[4718592]{0:T(1024)(128)(4,1)}), s8[4194304]{0:T(1024)(128)(4,1)S(1)}, s32[]{:S(2)}) async-start(s8[4718592]{0:T(1024)(128)(4,1)} %bitcast.892), calls=%async_computation.33 | async-start | bytes 8388608
  622.8 148.2 %copy-start.170 = (f32[256]{0:T(256)}, f32[256]{0:T(256)S(1)}, u32[]{:S(2)}) copy-start(f32[256]{0:T(256)S(1)} %get-tuple-element.1133) | copy-start | bytes 3076
  622.8 228.3 %copy-start.179 = (f32[256]{0:T(256)}, f32[256]{0:T(256)S(1)}, u32[]{:S(2)}) copy-start(f32[256]{0:T(256)S(1)} %get-tuple-element.1132) | copy-start | bytes 3076
  622.8 87.8 %copy-start.88 = (bf16[1,512,768]{2,1,0:T(8,128)(2,1)S(1)}, bf16[1,512,768]{2,1,0:T(8,128)(2,1)}, u32[]{:S(2)}) copy-start(bf16[1,512,768]{2,1,0:T(8,128)(2,1)} %param.32) | copy-start | bytes 2359300
  622.8 87.8 %slice-start.7 = ((s8[4718592]{0:T(1024)(128)(4,1)}), s8[524288]{0:T(1024)(128)(4,1)S(1)}, s32[]{:S(2)}) async-start(s8[4718592]{0:T(1024)(128)(4,1)} %bitcast.892), calls=%async_computation.34 | async-start | bytes 1048576
  624.4 95.8 %copy-start.215 = (f32[256,3072]{1,0:T(8,128)}, f32[256,3072]{1,0:T(8,128)S(1)}, u32[]{:S(2)}) copy-start(f32[256,3072]{1,0:T(8,128)S(1)} %fusion.138) | copy-start | bytes 9437188
  773.5 64.7 %collective-permute-start.3 = (bf16[256,768]{1,0:T(8,128)(2,1)S(1)}, bf16[256,768]{1,0:T(8,128)(2,1)S(1)}, u32[]{:S(2)}, u32[]{:S(2)}) collective-permute-start(bf16[256,768]{1,0:T(8,128)(2,1)S(1)} %get-tuple-element.1032), channel_id=1, source_target_pairs={{16,0},{17,1},{18,2},{19,3},{20,4},{21,5},{22,6},{23,7},{24,8},{25... | collective-permute-start | bytes 1179656 | tf_op jit(solution)/shard_map/ppermute | solution.py:25
  775.0 76.1 %copy-start.177 = (f32[256]{0:T(256)}, f32[256]{0:T(256)S(1)}, u32[]{:S(2)}) copy-start(f32[256]{0:T(256)S(1)} %add_rsqrt_fusion.7) | copy-start | bytes 3076
  775.0 63.1 %slice-start.8 = ((s8[4718592]{0:T(1024)(128)(4,1)}), s8[4194304]{0:T(1024)(128)(4,1)S(1)}, s32[]{:S(2)}) async-start(s8[4718592]{0:T(1024)(128)(4,1)} %bitcast.894), calls=%async_computation.35 | async-start | bytes 8388608
  781.5 67.4 %slice-start.14 = ((s8[4718592]{0:T(1024)(128)(4,1)}), s8[4194304]{0:T(1024)(128)(4,1)S(1)}, s32[]{:S(2)}) async-start(s8[4718592]{0:T(1024)(128)(4,1)} %bitcast.900), calls=%async_computation.41 | async-start | bytes 8388608
  785.4 63.5 %copy-start.181 = (f32[256]{0:T(256)S(1)}, f32[256]{0:T(256)}, u32[]{:S(2)}) copy-start(f32[256]{0:T(256)} %broadcast_multiply_fusion.14) | copy-start | bytes 3076
  785.4 63.4 %slice-start.15 = ((s8[4718592]{0:T(1024)(128)(4,1)}), s8[524288]{0:T(1024)(128)(4,1)S(1)}, s32[]{:S(2)}) async-start(s8[4718592]{0:T(1024)(128)(4,1)} %bitcast.900), calls=%async_computation.42 | async-start | bytes 1048576
  901.3 236.4 %reduce-scatter.35.cloned.1.call-start = ((), (), s32[]{:S(2)}) async-start(), calls=%async_computation.26 | async-start | bytes 417792
  905.7 233.4 %reduce-scatter.31.cloned.1.call-start = ((), (), s32[]{:S(2)}) async-start(), calls=%async_computation.24 | async-start | bytes 5308416
  921.6 303.0 %reduce-scatter.25.cloned.1.call-start = ((), (), s32[]{:S(2)}) async-start(), calls=%async_computation.21 | async-start | bytes 2433024 | tf_op jit(solution)/shard_map/reduce_scatter | solution.py:445
  926.1 402.2 %reduce-scatter.29.cloned.1.call-start = ((), (), s32[]{:S(2)}) async-start(), calls=%async_computation.23 | async-start | bytes 2433024 | tf_op jit(solution)/shard_map/reduce_scatter | solution.py:447
  930.6 464.7 %reduce-scatter.19.cloned.1.call-start = ((), (), s32[]{:S(2)}) async-start(), calls=%async_computation.18 | async-start | bytes 2506752 | tf_op jit(solution)/shard_map/reduce_scatter | solution.py:438
  950.8 556.4 %reduce-scatter.27.cloned.1.call-start = ((), (), s32[]{:S(2)}) async-start(), calls=%async_computation.22 | async-start | bytes 4866048 | tf_op jit(solution)/shard_map/reduce_scatter | solution.py:446
  958.5 642.8 %reduce-scatter.17.cloned.1.call-start = ((), (), s32[]{:S(2)}) async-start(), calls=%async_computation.17 | async-start | bytes 7520256 | tf_op jit(solution)/shard_map/reduce_scatter | solution.py:437
  971.0 745.8 %reduce-scatter.21.cloned.1.call-start = ((), (), s32[]{:S(2)}) async-start(), calls=%async_computation.19 | async-start | bytes 10027008 | tf_op jit(solution)/shard_map/reduce_scatter | solution.py:439
  984.2 848.8 %reduce-scatter.23.cloned.1.call-start = ((), (), s32[]{:S(2)}) async-start(), calls=%async_computation.20 | async-start | bytes 10027008 | tf_op jit(solution)/shard_map/reduce_scatter | solution.py:440
  1036.8 99.4 %copy-start.71 = (bf16[2,256,768]{2,1,0:T(8,128)(2,1)}, bf16[2,256,768]{2,1,0:T(8,128)(2,1)S(1)}, u32[]{:S(2)}) copy-start(bf16[2,256,768]{2,1,0:T(8,128)(2,1)S(1)} %fusion.409) | copy-start | bytes 2359300
  1036.9 97.4 %copy-start.194 = (f32[256]{0:T(256)S(1)}, f32[256]{0:T(256)}, u32[]{:S(2)}) copy-start(f32[256]{0:T(256)} %get-tuple-element.990) | copy-start | bytes 3076
  1036.9 97.3 %copy-start.193 = (f32[256]{0:T(256)S(1)}, f32[256]{0:T(256)}, u32[]{:S(2)}) copy-start(f32[256]{0:T(256)} %get-tuple-element.1017) | copy-start | bytes 3076
  1036.9 97.3 %copy-start.183 = (f32[256]{0:T(256)S(1)}, f32[256]{0:T(256)}, u32[]{:S(2)}) copy-start(f32[256]{0:T(256)} %broadcast_multiply_fusion.14) | copy-start | bytes 3076
  1036.9 97.3 %copy-start.186 = (f32[256]{0:T(256)S(1)}, f32[256]{0:T(256)}, u32[]{:S(2)}) copy-start(f32[256]{0:T(256)} %copy-done.184) | copy-start | bytes 3076
  (148 other events, 1096.7 us)
Sparse Core Ops, SparseCore 0:
  10.9 49.9 all-gather.7
  63.8 37.7 all-gather.9
  105.0 53.7 all-gather.13
  162.1 52.9 all-gather.15
  218.3 56.1 all-gather.11
  277.2 52.2 all-gather.19
  332.4 51.7 all-gather.17
  901.4 108.8 reduce-scatter.32
  1014.2 54.5 reduce-scatter.34
  1071.4 47.3 reduce-scatter.30
  1125.6 99.0 reduce-scatter.24
  1230.4 97.9 reduce-scatter.28
  1333.2 62.0 reduce-scatter.18
  1401.2 106.0 reduce-scatter.26
  1512.2 89.1 reduce-scatter.16
  1605.9 110.8 reduce-scatter.20
  1721.8 111.0 reduce-scatter.22
where the time goes:
time: 1850 us; the launch traced here: 1840 us
  waiting for transfers between devices  1090 us (59%)
  matrix products  213 us (12%)
  local copies, waits for them, and re-layouts  181 us (10%)
  blocking collectives  178 us (10%)
  other arithmetic  87.2 us (5%)
  starting transfers between devices  41.3 us (2%)
  loops' own time  36.9 us (2%)
    ppermute x4, waiting for transfers between devices, shifted(): return lax.ppermute(shard, axis, pairs)  154 us
    unnamed x2, blocking collectives  137 us
    reduce_scatter x1, waiting for transfers between devices, local(): lax.psum_scatter(layer_totals[5][None], 'dp', scatter_dimension=1, tiled=...  116 us
    reduce_scatter x1, waiting for transfers between devices, local(): lax.psum_scatter(layer_totals[4][None], 'dp', scatter_dimension=1, tiled=...  115 us
    reduce_scatter x1, waiting for transfers between devices, local(): lax.psum_scatter(cross_totals[3], ('section', 'dp'), scatter_dimension=0,...  112 us
    reduce_scatter x1, waiting for transfers between devices, local(): lax.psum_scatter(cross_totals[4], ('section', 'dp'), scatter_dimension=0,...  104 us
    reduce_scatter x1, waiting for transfers between devices, local(): lax.psum_scatter(layer_totals[2][None], 'dp', scatter_dimension=1, tiled=...  94.1 us
    dot_general x15, matrix products, matmul(): return jnp.dot(left, right, preferred_element_type=jnp.float32)  78.4 us
  transfers between devices with their start and end apart: 21, of which 16 were waited for; matrix products, arithmetic and copies ran while one was open for 11% of the time, Pallas kernels for 0%

commit v1 on v0

v1 whole, which is shorter than its diff:
```python
from functools import partial

import jax
import jax.numpy as jnp
import numpy as np
from jax import lax
from jax.experimental import pallas as pl
from jax.experimental.pallas import tpu as pltpu
from jax.sharding import PartitionSpec as P

HEADS = 12
HEAD_DIM = 64
PATCHES = 576
ROW_LEN = 64
SEGS = 3
IMG_MB = 2
ROWS_MB = 4
BLOCK = ROWS_MB * ROW_LEN
PAIR = 2 * HEAD_DIM
PAIRS = HEADS // 2
TILE = 2 * ROW_LEN
MASKED_SCORE = -1000000000.0
NORM_EPS = 1e-05
SCALE = HEAD_DIM ** (-0.5)
VMEM_LIMIT = 56 * 1024 * 1024

F32 = jnp.float32
BF16 = jnp.bfloat16


def dot(a, b):
    return lax.dot_general(a, b, (((1,), (0,)), ((), ())), preferred_element_type=F32)


def dot_nt(a, b):
    return lax.dot_general(a, b, (((1,), (1,)), ((), ())), preferred_element_type=F32)


def dot_tn(a, b):
    return lax.dot_general(a, b, (((0,), (0,)), ((), ())), preferred_element_type=F32)


def norm_parts(x):
    mean = jnp.mean(x, axis=-1, keepdims=True)
    centred = x - mean
    inv = lax.rsqrt(jnp.mean(centred * centred, axis=-1, keepdims=True) + NORM_EPS)
    return centred * inv, inv


def norm_back(d_out, normed, inv, gain):
    d_normed = d_out * gain
    d_input = inv * (
        d_normed
        - jnp.mean(d_normed, axis=-1, keepdims=True)
        - normed * jnp.mean(d_normed * normed, axis=-1, keepdims=True)
    )
    sums = jnp.concatenate(
        [
            jnp.sum(d_out * normed, axis=0, keepdims=True),
            jnp.sum(d_out, axis=0, keepdims=True),
            jnp.zeros((6, d_out.shape[1]), F32),
        ],
        axis=0,
    )
    return d_input, sums


def lane_masks(dtype):
    lane = lax.broadcasted_iota(jnp.int32, (1, PAIR), 1)
    even = (lane < HEAD_DIM).astype(F32)
    return even.astype(dtype), (1.0 - even).astype(dtype)


def softmax(scores):
    top = jnp.max(scores, axis=-1, keepdims=True)
    e = jnp.exp(scores - top)
    return (e * (1.0 / jnp.sum(e, axis=-1, keepdims=True))).astype(BF16)


def stack_heads(part, even, odd):
    return jnp.concatenate([part * even, part * odd], axis=0)


def self_fwd_kernel(x_ref, vec_ref, code_ref, code_row_ref, w_ref, x1_ref, h_ref, qkv_ref, p_ref, o_ref):
    d = x_ref.shape[1]
    x = x_ref[...].astype(F32)
    normed, _ = norm_parts(x)
    h = (normed * vec_ref[0:1, :] + vec_ref[1:2, :]).astype(BF16)
    h_ref[...] = h
    qkv_ref[...] = dot(h, w_ref[:, : 3 * d]).astype(BF16)
    even, odd = lane_masks(BF16)
    for t in range(BLOCK // TILE):
        rows = slice(t * TILE, (t + 1) * TILE)
        causal = lax.broadcasted_iota(jnp.int32, (TILE, TILE), 1) <= lax.broadcasted_iota(
            jnp.int32, (TILE, TILE), 0
        )
        allowed = (code_ref[rows, :] == code_row_ref[0, :, rows]) & causal
        for p in range(PAIRS):
            lanes = slice(p * PAIR, (p + 1) * PAIR)
            q = qkv_ref[rows, lanes] * jnp.asarray(SCALE, BF16)
            k2 = stack_heads(qkv_ref[rows, d + p * PAIR : d + (p + 1) * PAIR], even, odd)
            v2 = stack_heads(qkv_ref[rows, 2 * d + p * PAIR : 2 * d + (p + 1) * PAIR], even, odd)
            s = dot_nt(q, k2)
            probs = jnp.concatenate(
                [
                    softmax(jnp.where(allowed, s[:, :TILE], MASKED_SCORE)),
                    softmax(jnp.where(allowed, s[:, TILE:], MASKED_SCORE)),
                ],
                axis=1,
            )
            p_ref[rows, 2 * p * TILE : 2 * (p + 1) * TILE] = probs
            o_ref[rows, lanes] = dot(probs, v2).astype(BF16)
    x1_ref[...] = x + dot(o_ref[...], w_ref[:, 3 * d :])


def self_bwd_kernel(x_ref, dy_ref, vec_ref, qkv_ref, p_ref, w_ref, dx_ref, dyb_ref, dqkv_ref, sums_ref):
    d = x_ref.shape[1]
    dy = dy_ref[...]
    dyb = dy.astype(BF16)
    dyb_ref[...] = dyb
    d_mixed = dot_nt(dyb, w_ref[:, 3 * d :]).astype(BF16)
    even, odd = lane_masks(BF16)
    for t in range(BLOCK // TILE):
        rows = slice(t * TILE, (t + 1) * TILE)
        for p in range(PAIRS):
            lanes = slice(p * PAIR, (p + 1) * PAIR)
            q2 = stack_heads(qkv_ref[rows, lanes] * jnp.asarray(SCALE, BF16), even, odd)
            k2 = stack_heads(qkv_ref[rows, d + p * PAIR : d + (p + 1) * PAIR], even, odd)
            v2 = stack_heads(qkv_ref[rows, 2 * d + p * PAIR : 2 * d + (p + 1) * PAIR], even, odd)
            do = d_mixed[rows, lanes]
            do2 = stack_heads(do, even, odd)
            dp = dot_nt(do, v2)
            probs_e = p_ref[rows, 2 * p * TILE : (2 * p + 1) * TILE]
            probs_o = p_ref[rows, (2 * p + 1) * TILE : (2 * p + 2) * TILE]
            ds = []
            for probs, part in ((probs_e, dp[:, :TILE]), (probs_o, dp[:, TILE:])):
                pf = probs.astype(F32)
                term = pf * part
                ds.append((term - pf * jnp.sum(term, axis=-1, keepdims=True)).astype(BF16))
            dq = dot(jnp.concatenate(ds, axis=1), k2) * SCALE
            dk = dot_tn(jnp.concatenate(ds, axis=0), q2)
            dv = dot_tn(jnp.concatenate([probs_e, probs_o], axis=0), do2)
            dqkv_ref[rows, lanes] = dq.astype(BF16)
            dqkv_ref[rows, d + p * PAIR : d + (p + 1) * PAIR] = dk.astype(BF16)
            dqkv_ref[rows, 2 * d + p * PAIR : 2 * d + (p + 1) * PAIR] = dv.astype(BF16)
    dh = dot_nt(dqkv_ref[...], w_ref[:, : 3 * d])
    normed, inv = norm_parts(x_ref[...].astype(F32))
    d_input, sums = norm_back(dh, normed, inv, vec_ref[0:1, :])
    dx_ref[...] = dy + d_input
    sums_ref[0] = sums


def gelu_parts(u):
    phi = 0.5 + 0.5 * lax.erf(u * (0.5**0.5))
    slope = phi + u * (jnp.exp(-0.5 * (u * u)) * ((2.0 * np.pi) ** -0.5))
    return u * phi, slope


def ffn_fwd_kernel(x_ref, vec_ref, up_ref, down_ref, y_ref, m_ref, g_ref, slope_ref):
    d = x_ref.shape[1]
    ff = up_ref.shape[1]
    x = x_ref[...]
    normed, _ = norm_parts(x)
    m = (normed * vec_ref[0:1, :] + vec_ref[1:2, :]).astype(BF16)
    m_ref[...] = m
    acc = x
    for j in range(ff // d):
        cols = slice(j * d, (j + 1) * d)
        g, slope = gelu_parts(dot(m, up_ref[:, cols]))
        g = g.astype(BF16)
        g_ref[:, cols] = g
        slope_ref[:, cols] = slope.astype(BF16)
        acc = acc + dot(g, down_ref[cols, :])
    y_ref[...] = acc.astype(y_ref.dtype)


def ffn_bwd_kernel(x_ref, dy_ref, vec_ref, slope_ref, up_ref, down_ref, dx_ref, dyb_ref, du_ref, sums_ref):
    d = x_ref.shape[1]
    ff = up_ref.shape[1]
    dy = dy_ref[...].astype(F32)
    dyb = dy.astype(BF16)
    dyb_ref[...] = dyb
    acc = None
    for j in range(ff // d):
        cols = slice(j * d, (j + 1) * d)
        du = (dot_nt(dyb, down_ref[cols, :]) * slope_ref[:, cols].astype(F32)).astype(BF16)
        du_ref[:, cols] = du
        part = dot_nt(du, up_ref[:, cols])
        acc = part if acc is None else acc + part
    normed, inv = norm_parts(x_ref[...])
    d_input, sums = norm_back(acc, normed, inv, vec_ref[0:1, :])
    dx_ref[...] = dy + d_input
    sums_ref[0] = sums


def tied(part, first, second):
    return jnp.concatenate([part * first, part * second], axis=1)


def cross_fwd_kernel(x_ref, vec_ref, image_ref, kv_ref, w_ref, x2_ref, h_ref, q_ref, p_ref, o_ref):
    d = x_ref.shape[1]
    n = PATCHES
    x = x_ref[...]
    normed, _ = norm_parts(x)
    h = (normed * vec_ref[0:1, :] + vec_ref[1:2, :]).astype(BF16)
    h_ref[...] = h
    q_ref[...] = dot(h, w_ref[:, :d]).astype(BF16)
    even, odd = lane_masks(BF16)
    image = image_ref[...]
    second = image.astype(BF16)
    first = (1.0 - image).astype(BF16)
    lane_even = lax.broadcasted_iota(jnp.int32, (BLOCK, PAIR), 1) < HEAD_DIM
    is_first = jnp.broadcast_to(image, (BLOCK, PAIR)) < 0.5
    for p in range(PAIRS):
        lanes = slice(p * PAIR, (p + 1) * PAIR)
        vlanes = slice(d + p * PAIR, d + (p + 1) * PAIR)
        k2 = jnp.concatenate([kv_ref[:n, lanes], kv_ref[n:, lanes]], axis=1)
        v2 = jnp.concatenate([kv_ref[:n, vlanes], kv_ref[n:, vlanes]], axis=1)
        q = q_ref[:, lanes] * jnp.asarray(SCALE, BF16)
        out = []
        for half, mask in enumerate((even, odd)):
            probs = softmax(dot_nt(tied(q * mask, first, second), k2))
            p_ref[2 * p + half] = probs
            both = dot(probs, v2)
            out.append(jnp.where(is_first, both[:, :PAIR], both[:, PAIR:]))
        o_ref[:, lanes] = jnp.where(lane_even, out[0], out[1]).astype(BF16)
    x2_ref[...] = x + dot(o_ref[...], w_ref[:, 3 * d : 4 * d])


def cross_bwd_kernel(
    x_ref, dy_ref, vec_ref, image_ref, q_ref, p_ref, kv_ref, w_ref, dx_ref, dyb_ref, dq_ref, dkv_ref, sums_ref
):
    d = x_ref.shape[1]
    n = PATCHES
    dy = dy_ref[...]
    dyb = dy.astype(BF16)
    dyb_ref[...] = dyb
    d_mixed = dot_nt(dyb, w_ref[:, 3 * d : 4 * d]).astype(BF16)
    even, odd = lane_masks(BF16)
    image = image_ref[...]
    second = image.astype(BF16)
    first = (1.0 - image).astype(BF16)
    lane_even = lax.broadcasted_iota(jnp.int32, (BLOCK, PAIR), 1) < HEAD_DIM
    is_first = jnp.broadcast_to(image, (BLOCK, PAIR)) < 0.5
    for p in range(PAIRS):
        lanes = slice(p * PAIR, (p + 1) * PAIR)
        vlanes = slice(d + p * PAIR, d + (p + 1) * PAIR)
        k2 = jnp.concatenate([kv_ref[:n, lanes], kv_ref[n:, lanes]], axis=1)
        v2 = jnp.concatenate([kv_ref[:n, vlanes], kv_ref[n:, vlanes]], axis=1)
        q = q_ref[:, lanes] * jnp.asarray(SCALE, BF16)
        do = d_mixed[:, lanes]
        ds, qq, dd, dq = [], [], [], []
        for half, mask in enumerate((even, odd)):
            qq.append(tied(q * mask, first, second))
            dd.append(tied(do * mask, first, second))
            dp = dot_nt(dd[half], v2)
            pf = p_ref[2 * p + half].astype(F32)
            term = pf * dp
            ds.append((term - pf * jnp.sum(term, axis=-1, keepdims=True)).astype(BF16))
            both = dot(ds[half], k2)
            dq.append(jnp.where(is_first, both[:, :PAIR], both[:, PAIR:]))
        dq_ref[:, lanes] = (jnp.where(lane_even, dq[0], dq[1]) * SCALE).astype(BF16)
        dk = dot_tn(jnp.concatenate(ds, axis=0), jnp.concatenate(qq, axis=0)).astype(BF16)
        dv = dot_tn(
            jnp.concatenate([p_ref[2 * p], p_ref[2 * p + 1]], axis=0), jnp.concatenate(dd, axis=0)
        ).astype(BF16)
        dkv_ref[:n, lanes] = dk[:, :PAIR]
        dkv_ref[n:, lanes] = dk[:, PAIR:]
        dkv_ref[:n, vlanes] = dv[:, :PAIR]
        dkv_ref[n:, vlanes] = dv[:, PAIR:]
    dh = dot_nt(dq_ref[...], w_ref[:, :d])
    normed, inv = norm_parts(x_ref[...])
    d_input, sums = norm_back(dh, normed, inv, vec_ref[0:1, :])
    dx_ref[...] = dy + d_input
    sums_ref[0] = sums


def rows_spec(rows, cols):
    return pl.BlockSpec((rows, cols), lambda i: (i, 0))


def whole_spec(shape):
    return pl.BlockSpec(shape, lambda i: (0,) * len(shape), pipeline_mode=pl.Buffered(1))


def call(kernel, blocks, in_specs, out_specs, out_shape, flops, moved, trans=0):
    return pl.pallas_call(
        kernel,
        grid=(blocks,),
        in_specs=in_specs,
        out_specs=out_specs,
        out_shape=out_shape,
        compiler_params=pltpu.CompilerParams(vmem_limit_bytes=VMEM_LIMIT),
        cost_estimate=pl.CostEstimate(flops=flops, bytes_accessed=moved, transcendentals=trans),
    )


def sds(shape, dtype):
    return jax.ShapeDtypeStruct(shape, dtype)


def sums_spec(d):
    return pl.BlockSpec((1, 8, d), lambda i: (i, 0, 0))


def self_fwd(x, vec, code, code_row, w):
    t, d = x.shape
    nb = t // BLOCK
    return call(
        self_fwd_kernel,
        nb,
        [
            rows_spec(BLOCK, d),
            whole_spec((8, d)),
            rows_spec(BLOCK, 1),
            pl.BlockSpec((1, 1, BLOCK), lambda i: (i, 0, 0)),
            whole_spec((d, 4 * d)),
        ],
        [
            rows_spec(BLOCK, d),
            rows_spec(BLOCK, d),
            rows_spec(BLOCK, 3 * d),
            rows_spec(BLOCK, HEADS * TILE),
            rows_spec(BLOCK, d),
        ],
        [
            sds((t, d), F32),
            sds((t, d), BF16),
            sds((t, 3 * d), BF16),
            sds((t, HEADS * TILE), BF16),
            sds((t, d), BF16),
        ],
        t * d * 8 * d + t * HEADS * TILE * 512,
        d * d * 8 + t * d * 24,
    )(x, vec, code, code_row, w)


def self_bwd(x, dy, vec, qkv, probs, w):
    t, d = x.shape
    nb = t // BLOCK
    return call(
        self_bwd_kernel,
        nb,
        [
            rows_spec(BLOCK, d),
            rows_spec(BLOCK, d),
            whole_spec((8, d)),
            rows_spec(BLOCK, 3 * d),
            rows_spec(BLOCK, HEADS * TILE),
            whole_spec((d, 4 * d)),
        ],
        [rows_spec(BLOCK, d), rows_spec(BLOCK, d), rows_spec(BLOCK, 3 * d), sums_spec(d)],
        [sds((t, d), F32), sds((t, d), BF16), sds((t, 3 * d), BF16), sds((nb, 8, d), F32)],
        t * d * 8 * d + t * HEADS * TILE * 1024,
        d * d * 8 + t * d * 30,
    )(x, dy, vec, qkv, probs, w)


def ffn_fwd(x, vec, up, down, out_dtype):
    t, d = x.shape
    ff = up.shape[1]
    nb = t // BLOCK
    return call(
        ffn_fwd_kernel,
        nb,
        [rows_spec(BLOCK, d), whole_spec((8, d)), whole_spec((d, ff)), whole_spec((ff, d))],
        [rows_spec(BLOCK, d), rows_spec(BLOCK, d), rows_spec(BLOCK, ff), rows_spec(BLOCK, ff)],
        [sds((t, d), out_dtype), sds((t, d), BF16), sds((t, ff), BF16), sds((t, ff), BF16)],
        t * d * 4 * ff,
        d * ff * 4 + t * (d * 8 + ff * 4),
        2 * t * ff,
    )(x, vec, up, down)


def ffn_bwd(x, dy, vec, slope, up, down):
    t, d = x.shape
    ff = up.shape[1]
    nb = t // BLOCK
    return call(
        ffn_bwd_kernel,
        nb,
        [
            rows_spec(BLOCK, d),
            rows_spec(BLOCK, d),
            whole_spec((8, d)),
            rows_spec(BLOCK, ff),
            whole_spec((d, ff)),
            whole_spec((ff, d)),
        ],
        [rows_spec(BLOCK, d), rows_spec(BLOCK, d), rows_spec(BLOCK, ff), sums_spec(d)],
        [sds((t, d), F32), sds((t, d), BF16), sds((t, ff), BF16), sds((nb, 8, d), F32)],
        t * d * 4 * ff,
        d * ff * 4 + t * (d * 14 + ff * 4),
    )(x, dy, vec, slope, up, down)


def cross_fwd(x, vec, image, kv, w):
    t, d = x.shape
    nb = t // BLOCK
    wide = w.shape[1]
    return call(
        cross_fwd_kernel,
        nb,
        [
            rows_spec(BLOCK, d),
            whole_spec((8, d)),
            rows_spec(BLOCK, 1),
            rows_spec(IMG_MB * PATCHES, 2 * d),
            whole_spec((d, wide)),
        ],
        [
            rows_spec(BLOCK, d),
            rows_spec(BLOCK, d),
            rows_spec(BLOCK, d),
            pl.BlockSpec((HEADS, BLOCK, PATCHES), lambda i: (i, 0, 0)),
            rows_spec(BLOCK, d),
        ],
        [
            sds((t, d), F32),
            sds((t, d), BF16),
            sds((t, d), BF16),
            sds((nb * HEADS, BLOCK, PATCHES), BF16),
            sds((t, d), BF16),
        ],
        t * d * 4 * d + 4 * t * HEADS * PATCHES * 256,
        d * d * 8 + t * d * 16 + nb * PATCHES * d * 8 + t * HEADS * PATCHES * 2,
        t * HEADS * PATCHES,
    )(x, vec, image, kv, w)


def cross_bwd(x, dy, vec, image, q, probs, kv, w):
    t, d = x.shape
    nb = t // BLOCK
    wide = w.shape[1]
    return call(
        cross_bwd_kernel,
        nb,
        [
            rows_spec(BLOCK, d),
            rows_spec(BLOCK, d),
            whole_spec((8, d)),
            rows_spec(BLOCK, 1),
            rows_spec(BLOCK, d),
            pl.BlockSpec((HEADS, BLOCK, PATCHES), lambda i: (i, 0, 0)),
            rows_spec(IMG_MB * PATCHES, 2 * d),
            whole_spec((d, wide)),
        ],
        [
            rows_spec(BLOCK, d),
            rows_spec(BLOCK, d),
            rows_spec(BLOCK, d),
            rows_spec(IMG_MB * PATCHES, 2 * d),
            sums_spec(d),
        ],
        [
            sds((t, d), F32),
            sds((t, d), BF16),
            sds((t, d), BF16),
            sds((nb * IMG_MB * PATCHES, 2 * d), BF16),
            sds((nb, 8, d), F32),
        ],
        t * d * 4 * d + 8 * t * HEADS * PATCHES * 256,
        d * d * 8 + t * d * 16 + nb * PATCHES * d * 16 + t * HEADS * PATCHES * 2,
    )(x, dy, vec, image, q, probs, kv, w)


CORES = 2
RING = 8


def ring_tables():
    half = RING // 2
    chip_at = [2 * z for z in range(half)] + [2 * z + 1 for z in range(half - 1, -1, -1)]
    pos_of = [chip_at.index(chip) for chip in range(RING)]
    return chip_at, pos_of


CHIP_AT, POS_OF = ring_tables()


def flat(section, chip, core):
    return section * RING * CORES + chip * CORES + core


def ring_pairs(sections, step):
    return [
        (flat(s, CHIP_AT[i], c), flat(s, CHIP_AT[(i + step) % RING], c))
        for s in sections
        for i in range(RING)
        for c in range(CORES)
    ]


def core_pairs(sections):
    return [
        (flat(s, chip, c), flat(s, chip, 1 - c))
        for s in sections
        for chip in range(RING)
        for c in range(CORES)
    ]


def send(x, pairs):
    return lax.ppermute(x, ("section", "dp"), pairs)


def tie(x, deps):
    if not deps:
        return x
    return lax.optimization_barrier((x, *deps))[0]


def place(chip_count):
    return lax.axis_index("dp") // CORES, lax.axis_index("dp") % CORES


def chip_by_offset(offset):
    pos = jnp.asarray(POS_OF, jnp.int32)[lax.axis_index("dp") // CORES]
    return jnp.asarray(CHIP_AT, jnp.int32)[(pos + offset + RING) % RING]


def ring_gather(chunk, sections, long_way, deps, by_core):
    core = lax.axis_index("dp") % CORES
    first, second = (CORES, RING) if by_core else (RING, CORES)
    whole = jnp.zeros((first, second) + chunk.shape, chunk.dtype)

    def put(whole, piece, offset, piece_core):
        chip = chip_by_offset(offset)
        start = (piece_core, chip) if by_core else (chip, piece_core)
        return lax.dynamic_update_slice(whole, piece[None, None], start + (0,) * chunk.ndim)

    def keep(whole, piece, offset):
        whole = put(whole, piece, offset, core)
        return put(whole, send(piece, core_pairs(sections)), offset, 1 - core)

    chunk = tie(chunk, deps)
    arrivals = {1: [], -1: []}
    for step in range(1, RING // 2 + 1):
        for way in (1, -1):
            if step == RING // 2 and way != long_way:
                continue
            held = arrivals[way][-1] if arrivals[way] else chunk
            arrivals[way].append(send(held, ring_pairs(sections, way)))
    whole = keep(whole, chunk, 0)
    for step in range(1, RING // 2 + 1):
        for way in (1, -1):
            if step <= len(arrivals[way]):
                whole = keep(whole, arrivals[way][step - 1], -way * step)
    return whole.reshape((RING * CORES * chunk.shape[0],) + chunk.shape[1:]), arrivals


def ring_scatter(partial_sums, sections, long_way, by_core):
    core = lax.axis_index("dp") % CORES
    rows = partial_sums.shape[0] // (RING * CORES)
    first, second = (CORES, RING) if by_core else (RING, CORES)
    axis = 0 if by_core else 1
    split = partial_sums.reshape((first, second, rows) + partial_sums.shape[1:])
    theirs = lax.dynamic_index_in_dim(split, 1 - core, axis, keepdims=False)
    mine = lax.dynamic_index_in_dim(split, core, axis, keepdims=False)
    joined = (mine.astype(F32) + send(theirs, core_pairs(sections)).astype(F32)).astype(BF16)

    def own(offset):
        return lax.dynamic_index_in_dim(joined, chip_by_offset(offset), 0, keepdims=False)

    total = own(0).astype(F32)
    for way in (1, -1):
        hops = RING // 2 if way == long_way else RING // 2 - 1
        moving = None
        for step in range(hops):
            piece = own(way * (hops - step))
            if moving is not None:
                piece = (piece.astype(F32) + moving.astype(F32)).astype(BF16)
            moving = send(piece, ring_pairs(sections, way))
        total = total + moving.astype(F32)
    return total


def vec_rows(gain, bias):
    rows = jnp.stack([gain, bias]).astype(F32)
    return jnp.concatenate([rows, jnp.zeros((6, rows.shape[1]), F32)], axis=0)


def lanes_of(vectors, width):
    table = jnp.stack(vectors, axis=1)
    return jnp.pad(table, ((0, 0), (0, width - table.shape[1])))


def local(
    tokens,
    images,
    segments,
    image_ids,
    cotangent,
    norm_gain,
    norm_bias,
    qkv_weight,
    out_weight,
    up_weight,
    down_weight,
    cross_gain,
    cross_bias,
    cross_query,
    cross_kv,
    cross_out,
):
    section = lax.axis_index("section")
    multimodal = section == 1
    d = tokens.shape[1]
    t = tokens.shape[0]
    nb = t // BLOCK
    members = lax.axis_size("dp")
    ringed = members == RING * CORES and lax.axis_size("section") == 2

    attn_piece = jnp.concatenate(
        [
            qkv_weight[0],
            out_weight[0],
            lanes_of([norm_gain[0, 0], norm_bias[0, 0], norm_gain[0, 1], norm_bias[0, 1]], PAIR),
        ],
        axis=1,
    ).astype(BF16)
    up_piece = up_weight[0].astype(BF16)
    down_piece = down_weight[0].astype(BF16)
    cross_piece = jnp.concatenate(
        [cross_query, cross_kv, cross_out, lanes_of([cross_gain, cross_bias], PAIR)], axis=1
    ).astype(BF16)

    if ringed:
        core = lax.axis_index("dp") % CORES
        both = (0, 1)
        one = send(
            cross_piece,
            [(flat(0, k, 0), flat(1, k, 0)) for k in range(RING)]
            + [(flat(1, k, 0), flat(1, k, 1)) for k in range(RING)],
        )
        two = send(cross_piece, [(flat(0, k, 1), flat(1, k, 0)) for k in range(RING)])
        cross_chunk = jnp.concatenate([one, jnp.where(core == 0, two, cross_piece)], axis=0)
        w_attn, seen = ring_gather(attn_piece, both, 1, (), False)
        w_cross, seen_cross = ring_gather(cross_chunk, (1,), -1, (seen[1][1],), True)
        w_up, seen_up = ring_gather(up_piece, both, -1, (seen[1][1], seen[-1][1]), False)
        w_down, _ = ring_gather(down_piece, both, 1, (seen_up[1][1], seen_up[-1][1]), False)
    else:
        w_attn = lax.all_gather(attn_piece, "dp", axis=0, tiled=True)
        w_up = lax.all_gather(up_piece, "dp", axis=0, tiled=True)
        w_down = lax.all_gather(down_piece, "dp", axis=0, tiled=True)
        w_cross = lax.all_gather(cross_piece, ("section", "dp"), axis=0, tiled=True)

    vec_table = w_attn[:, 4 * d : 4 * d + 4].T
    vec_attn = vec_rows(vec_table[0], vec_table[1])
    vec_ffn = vec_rows(vec_table[2], vec_table[3])
    cross_table = w_cross[:, 4 * d : 4 * d + 2].T
    vec_cross = vec_rows(cross_table[0], cross_table[1])

    row_in_tile = lax.broadcasted_iota(jnp.int32, segments.shape, 0) % (TILE // ROW_LEN)
    code = (row_in_tile * (SEGS + 1) + segments).reshape(-1)
    code_col = code[:, None]
    code_row = code.reshape(nb, 1, BLOCK)
    slots = lax.broadcasted_iota(jnp.int32, (1, 1, SEGS), 2)
    token_image = jnp.sum(
        jnp.where(segments[:, :, None] == slots, image_ids[:, None, :], 0), axis=-1
    )
    image_col = token_image.reshape(-1, 1).astype(F32)
    patches = images.reshape(-1, d)

    kv = dot(patches, w_cross[:, d : 3 * d]).astype(BF16)

    a_x1, a_h, a_qkv, a_p, a_o = self_fwd(tokens, vec_attn, code_col, code_row, w_attn)
    a_y, a_m, a_g, a_slope = [], [], [], []
    for b in range(nb):
        rows = slice(b * BLOCK, (b + 1) * BLOCK)
        for got, part in zip(
            (a_y, a_m, a_g, a_slope), ffn_fwd(a_x1[rows], vec_ffn, w_up, w_down, BF16)
        ):
            got.append(part)
    arriving = jnp.concatenate([lax.ppermute(y, "section", [(0, 1)]) for y in a_y])
    a_y, a_m, a_g, a_slope = (jnp.concatenate(parts) for parts in (a_y, a_m, a_g, a_slope))

    b_x1, b_h, b_qkv, b_p, b_o = self_fwd(arriving, vec_attn, code_col, code_row, w_attn)
    b_x2, c_h, c_q, c_p, c_o = cross_fwd(b_x1, vec_cross, image_col, kv, w_cross)
    b_y, b_m, b_g, b_slope = ffn_fwd(b_x2, vec_ffn, w_up, w_down, BF16)
    b_dx2, b_dy, b_du, b_fsum = ffn_bwd(b_x2, cotangent[0], vec_ffn, b_slope, w_up, w_down)
    b_dx1, c_dy, c_dq, c_dkv, c_sum = cross_bwd(
        b_x1, b_dx2, vec_cross, image_col, c_q, c_p, kv, w_cross
    )
    b_dx0, b_dy1, b_dqkv, b_asum = self_bwd(arriving, b_dx1, vec_attn, b_qkv, b_p, w_attn)
    returning = lax.ppermute(b_dx0.astype(BF16), "section", [(1, 0)])

    def low_tn(left, right):
        return dot_tn(left, right).astype(BF16)

    def attn_grads(h, dqkv, o, dyb, asum, fsum):
        sums = jnp.concatenate([jnp.sum(asum, axis=0)[:2], jnp.sum(fsum, axis=0)[:2]])
        columns = jnp.pad(sums.T, ((0, 0), (0, PAIR - 4))).astype(BF16)
        return jnp.concatenate([low_tn(h, dqkv), low_tn(o, dyb), columns], axis=1)

    def cross_grads():
        columns = jnp.pad(jnp.sum(c_sum, axis=0)[:2].T, ((0, 0), (0, PAIR - 2))).astype(BF16)
        return jnp.concatenate(
            [low_tn(c_h, c_dq), low_tn(patches, c_dkv), low_tn(c_o, c_dy), columns], axis=1
        )

    w_kv = w_cross[:, d : 3 * d]
    half = d // 2
    image_theirs = dot_nt(c_dkv, w_kv[:half]).astype(BF16)
    image_mine = dot_nt(c_dkv, w_kv[half:])
    image_shard = jnp.where(
        multimodal,
        image_mine,
        lax.ppermute(image_theirs, "section", [(1, 0)]).astype(F32),
    )

    a_dy_in = cotangent[0].astype(F32) + returning.astype(F32)
    a_dx1, a_dy, a_du, a_fsum = ffn_bwd(a_x1, a_dy_in, vec_ffn, a_slope, w_up, w_down)
    a_dx0, a_dy1, a_dqkv, a_asum = self_bwd(tokens, a_dx1, vec_attn, a_qkv, a_p, w_attn)

    b_down, b_up = low_tn(b_g, b_dy), low_tn(b_m, b_du)
    b_attn = attn_grads(b_h, b_dqkv, b_o, b_dy1, b_asum, b_fsum)
    b_cross = cross_grads()
    a_down, a_up = low_tn(a_g, a_dy), low_tn(a_m, a_du)
    a_attn = attn_grads(a_h, a_dqkv, a_o, a_dy1, a_asum, a_fsum)

    if ringed:
        s1, s0 = (1,), (0,)
        b_shards = [
            ring_scatter(b_down, s1, 1, False),
            ring_scatter(b_up, s1, -1, False),
            ring_scatter(b_attn, s1, -1, False),
        ]
        cross_sum = ring_scatter(b_cross, s1, 1, True)
        a_shards = [
            ring_scatter(a_down, s0, 1, False),
            ring_scatter(a_up, s0, -1, False),
            ring_scatter(a_attn, s0, 1, False),
        ]
        down_g, up_g, attn_g = (
            jnp.where(multimodal, second, first) for first, second in zip(a_shards, b_shards)
        )
        part = cross_sum.shape[0] // 2
        one = send(
            cross_sum[:part],
            [(flat(1, k, 0), flat(0, k, 0)) for k in range(RING)]
            + [(flat(1, k, 1), flat(1, k, 0)) for k in range(RING)],
        )
        two = send(cross_sum[part:], [(flat(1, k, 0), flat(0, k, 1)) for k in range(RING)])
        cross_g = jnp.where(
            core == 0, one, jnp.where(multimodal, cross_sum[part:], two)
        )
    else:
        def summed(first, second):
            return lax.psum_scatter(
                jnp.where(multimodal, second, first).astype(F32), "dp", scatter_dimension=0, tiled=True
            )

        down_g, up_g, attn_g = summed(a_down, b_down), summed(a_up, b_up), summed(a_attn, b_attn)
        cross_g = lax.psum_scatter(
            jnp.where(multimodal, b_cross, 0.0).astype(F32),
            ("section", "dp"),
            scatter_dimension=0,
            tiled=True,
        )

    vec_g = attn_g[:, 4 * d : 4 * d + 4].T
    return (
        jnp.where(multimodal, b_y, a_y)[None],
        jnp.where(multimodal, b_dx0, a_dx0)[None],
        image_shard.reshape(images.shape[0], images.shape[1], half),
        jnp.stack([vec_g[0], vec_g[2]])[None],
        jnp.stack([vec_g[1], vec_g[3]])[None],
        attn_g[None, :, : 3 * d],
        attn_g[None, :, 3 * d : 4 * d],
        up_g[None],
        down_g[None],
        cross_g[:, 4 * d],
        cross_g[:, 4 * d + 1],
        cross_g[:, :d],
        cross_g[:, d : 3 * d],
        cross_g[:, 3 * d : 4 * d],
    )


def solution(mesh):
    in_specs = (
        P("dp", None),
        P("dp", None, None),
        P("dp", None),
        P("dp", None),
        P("section", "dp", None),
        P("section", None, "dp"),
        P("section", None, "dp"),
        P("section", "dp", None),
        P("section", "dp", None),
        P("section", "dp", None),
        P("section", "dp", None),
        P(("section", "dp")),
        P(("section", "dp")),
        P(("section", "dp"), None),
        P(("section", "dp"), None),
        P(("section", "dp"), None),
    )
    out_specs = (
        P("section", "dp", None),
        P("section", "dp", None),
        P("dp", None, "section"),
        P("section", None, "dp"),
        P("section", None, "dp"),
        P("section", "dp", None),
        P("section", "dp", None),
        P("section", "dp", None),
        P("section", "dp", None),
        P(("section", "dp")),
        P(("section", "dp")),
        P(("section", "dp"), None),
        P(("section", "dp"), None),
        P(("section", "dp"), None),
    )
    return jax.shard_map(local, mesh=mesh, in_specs=in_specs, out_specs=out_specs, check_vma=False)
```

time: 1850 us -> 754 us (0.41)
  waiting for transfers between devices: 1090 us -> 164 us
  blocking collectives: 178 us -> 0 us
  matrix products: 213 us -> 58.5 us
  Pallas kernels: 0 us -> 142 us
  starting transfers between devices: 41.3 us -> 171 us
  local copies, waits for them, and re-layouts: 181 us -> 122 us
  loops' own time: 36.9 us -> 0 us
  other arithmetic: 87.2 us -> 56.2 us
    reduce_scatter x7 -> x0, waiting for transfers between devices: 683 us -> none  [the longest x1 116 us: local(): lax.psum_scatter(layer_totals[5][None], 'dp', scatter_dimension=1, tiled=...]
    all_gather x7 -> x0, waiting for transfers between devices: 248 us -> none  [the longest x1 59.5 us: local(): lax.all_gather(cross_kv.astype(jnp.bfloat16), ('section', 'dp'), axis=0,...]
    dot_general x63 -> x14, matrix products: 213 us -> 58.5 us  [the longest x11 33.8 us: dot_tn(): lax.dot_general(a, b, (((0,), (0,)), ((), ())), preferred_element_type=F32)]
    pallas_call x0 -> x11, Pallas kernels: none -> 142 us  [the longest x2 32.5 us: self_bwd(): call(self_bwd_kernel, nb, [rows_spec(BLOCK, d), rows_spec(BLOCK, d), whol...]
    unnamed x2 -> x0, blocking collectives: 137 us -> none
    ppermute x4 -> x124, starting transfers between devices: 39.8 us -> 171 us  [the longest x120 144 us: send(): return lax.ppermute(x, ('section', 'dp'), pairs)]
    dynamic_update_slice x0 -> x63, local copies, waits for them, and re-layouts: none -> 55.2 us  [put(): lax.dynamic_update_slice(whole, piece[None, None], start + (0,) * chunk.n...]
    all_gather x2 -> x0, blocking collectives: 41.3 us -> none  [the longest x1 22.5 us: local(): lax.all_gather(norm_bias.astype(jnp.bfloat16), 'dp', axis=2, tiled=True)]
  transfers between devices with their start and end apart: 21 -> 124, of which waited for: 16 -> 24; matrix products, arithmetic and copies ran while one was open for 11% -> 26% of each run, Pallas kernels for 0% -> 6%
where the time goes in v1:
time: 754 us; the launch traced here: 741 us
  starting transfers between devices  171 us (23%)
  waiting for transfers between devices  164 us (22%)
  Pallas kernels  142 us (19%)
  local copies, waits for them, and re-layouts  122 us (16%)
  matrix products  58.5 us (8%)
  other arithmetic  56.2 us (7%)
  between operations  26.7 us (4%)
    ppermute x120, waiting for transfers between devices, send(): return lax.ppermute(x, ('section', 'dp'), pairs)  158 us
    ppermute x120, starting transfers between devices, send(): return lax.ppermute(x, ('section', 'dp'), pairs)  144 us
    dynamic_update_slice x63, local copies, waits for them, and re-layouts, put(): lax.dynamic_update_slice(whole, piece[None, None], start + (0,) * chunk.n...  55.2 us
    dot_general x11, matrix products, dot_tn(): lax.dot_general(a, b, (((0,), (0,)), ((), ())), preferred_element_type=F32)  33.8 us
    pallas_call x2, Pallas kernels, self_bwd(): call(self_bwd_kernel, nb, [rows_spec(BLOCK, d), rows_spec(BLOCK, d), whol...  32.5 us
    pallas_call x3, Pallas kernels, ffn_fwd(): call(ffn_fwd_kernel, nb, [rows_spec(BLOCK, d), whole_spec((8, d)), whole_...  30 us
    pallas_call x2, Pallas kernels, ffn_bwd(): call(ffn_bwd_kernel, nb, [rows_spec(BLOCK, d), rows_spec(BLOCK, d), whole...  24.4 us
    ppermute x2, starting transfers between devices, local(): lax.ppermute(y, 'section', [(0, 1)])  24.2 us
  transfers between devices with their start and end apart: 124, of which 24 were waited for; matrix products, arithmetic and copies ran while one was open for 26% of the time, Pallas kernels for 6%

profile of v1, /device:TPU:0, one launch (start us, length us, event | category | flops | bytes accessed | tf_op | source)
XLA Modules:
  0.0 741.0 jit_solution(15594596469729503566)
XLA Ops:
  7.1 5.5 collective-permute-start.47
  64.1 4.7 collective-permute-done.7
  90.6 7.0 collective-permute-done.9
  103.5 3.7 collective-permute-done.20
  127.6 8.5 %collective-permute-done.24 = bf16[48,3072]{1,0:T(8,128)(2,1)} collective-permute-done((bf16[48,3072]{1,0:T(8,128)(2,1)S(1)}, bf16[48,3072]{1,0:T(8,128)(2,1)}, u32[]{:S(2)}, u32[]{:S(2)}) %collective-permute-start.24) | collective-permute-done | bytes 294944 | tf_op jit(solution)/shard_map/ppermute | solution.py:504
  155.6 9.9 %shard_map.2423 = (f32[512,768]{1,0:T(8,128)}, bf16[512,768]{1,0:T(8,128)(2,1)}, bf16[512,2304]{1,0:T(8,128)(2,1)}, bf16[512,1536]{1,0:T(8,128)(2,1)}, bf16[512,768]{1,0:T(8,128)(2,1)}) custom-call(bf16[512,768]{1,0:T(8,128)(2,1)} %x_ref.3, f32[8,768]{1,0:T(8,128)} %copy.435.vec_ref, s32[512,1]{1,0:T(8,128)} %broadcast_in_dim_reshape.4.code_ref, ...), custom_call_target="tpu_custom_call" | custom-call | flops 2818572288 | bytes 14155776 | tf_op jit(solution)/shard_map/pallas_call | solution.py:309
  195.1 5.8 collective-permute-done.39
  209.1 9.3 %fusion.3.kv_ref = bf16[2304,1536]{1,0:T(8,128)(2,1)} fusion(bf16[2304,768]{1,0:T(8,128)(2,1)S(1)} %bitcast.439, bf16[768,3200]{1,0:T(8,128)(2,1)} %bitcast.98.w_ref), kind=kOutput, calls=%fused_computation.6 | convolution fusion | flops 5439356928 | bytes 12976128 | tf_op jit(solution)/shard_map/dot_general | solution.py:32
  229.5 8.8 %shard_map.2425 = (bf16[256,768]{1,0:T(8,128)(2,1)}, bf16[256,768]{1,0:T(8,128)(2,1)}, bf16[256,3072]{1,0:T(8,128)(2,1)}, bf16[256,3072]{1,0:T(8,128)(2,1)}) custom-call(f32[256,768]{1,0:T(8,128)} %get-tuple-element.160.x_ref, f32[8,768]{1,0:T(8,128)} %copy.437.vec_ref, bf16[768,3072]{1,0:T(8,128)(2,1)} %bitcast.61.up_ref, bf16[3072,768]{1,0:T(8,128)(2,1)} %bitcast.79.down_ref), custom_call_target="tpu_custom_call" | custom-call | flops 2415919104 | bytes 14155776 | tf_op jit(solution)/shard_map/pallas_call | solution.py:363
  238.3 22.5 %collective-permute-start.46 = (bf16[256,768]{1,0:T(8,128)(2,1)}, bf16[256,768]{1,0:T(8,128)(2,1)S(1)}, u32[]{:S(2)}, u32[]{:S(2)}) collective-permute-start(bf16[256,768]{1,0:T(8,128)(2,1)} %get-tuple-element.69), channel_id=1, source_target_pairs={{0,16},{1,17},{2,18},{3,19},{4,20},{5,21},{6,22},{7,23},{8,24},{9,... | collective-permute-start | bytes 1179656 | tf_op jit(solution)/shard_map/ppermute | solution.py:675
  260.8 8.9 %shard_map.2424 = (bf16[256,768]{1,0:T(8,128)(2,1)}, bf16[256,768]{1,0:T(8,128)(2,1)}, bf16[256,3072]{1,0:T(8,128)(2,1)}, bf16[256,3072]{1,0:T(8,128)(2,1)}) custom-call(f32[256,768]{1,0:T(8,128)} %get-tuple-element.161.x_ref, f32[8,768]{1,0:T(8,128)} %copy.437.vec_ref, bf16[768,3072]{1,0:T(8,128)(2,1)} %bitcast.61.up_ref, bf16[3072,768]{1,0:T(8,128)(2,1)} %bitcast.79.down_ref), custom_call_target="tpu_custom_call" | custom-call | flops 2415919104 | bytes 14155776 | tf_op jit(solution)/shard_map/pallas_call | solution.py:363
  271.5 3.3 pad_maximum_fusion.slope_ref
  274.8 5.5 collective-permute-done.45
  281.2 9.8 %shard_map.2426 = (f32[512,768]{1,0:T(8,128)}, bf16[512,768]{1,0:T(8,128)(2,1)}, bf16[512,2304]{1,0:T(8,128)(2,1)}, bf16[512,1536]{1,0:T(8,128)(2,1)}, bf16[512,768]{1,0:T(8,128)(2,1)}) custom-call(bf16[512,768]{1,0:T(8,128)(2,1)} %copy-done.31, f32[8,768]{1,0:T(8,128)} %copy.435.vec_ref, s32[512,1]{1,0:T(8,128)} %broadcast_in_dim_reshape.4.code_ref, ...), custom_call_target="tpu_custom_call" | custom-call | flops 2818572288 | bytes 14155776 | tf_op jit(solution)/shard_map/pallas_call | solution.py:309
  291.0 14.7 %shard_map.2427 = (f32[512,768]{1,0:T(8,128)}, bf16[512,768]{1,0:T(8,128)(2,1)}, bf16[512,768]{1,0:T(8,128)(2,1)}, bf16[24,256,576]{2,1,0:T(8,128)(2,1)}, bf16[512,768]{1,0:T(8,128)(2,1)}) custom-call(f32[512,768]{1,0:T(8,128)} %get-tuple-element.70.x_ref, f32[8,768]{1,0:T(8,128)} %copy.443.vec_ref, f32[512,1]{1,0:T(8,128)} %convert_element_type.959.image_ref, ...), custom_call_target="tpu_custom_call" | custom-call | flops 4831838208 | bytes 25165824 | tf_op jit(solution)/shard_map/pallas_call | solution.py:401
  305.8 12.3 %shard_map.2428 = (bf16[512,768]{1,0:T(8,128)(2,1)}, bf16[512,768]{1,0:T(8,128)(2,1)}, bf16[512,3072]{1,0:T(8,128)(2,1)}, bf16[512,3072]{1,0:T(8,128)(2,1)}) custom-call(f32[512,768]{1,0:T(8,128)} %get-tuple-element.72.x_ref, f32[8,768]{1,0:T(8,128)} %copy.437.vec_ref, bf16[768,3072]{1,0:T(8,128)(2,1)} %bitcast.61.up_ref, bf16[3072,768]{1,0:T(8,128)(2,1)} %bitcast.79.down_ref), custom_call_target="tpu_custom_call" | custom-call | flops 4831838208 | bytes 18874368 | tf_op jit(solution)/shard_map/pallas_call | solution.py:363
  318.0 12.2 %shard_map.2429 = (f32[512,768]{1,0:T(8,128)}, bf16[512,768]{1,0:T(8,128)(2,1)}, bf16[512,3072]{1,0:T(8,128)(2,1)}, f32[2,8,768]{2,1,0:T(8,128)}) custom-call(f32[512,768]{1,0:T(8,128)} %get-tuple-element.72.x_ref, bf16[512,768]{1,0:T(8,128)(2,1)} %bitcast.468, f32[8,768]{1,0:T(8,128)} %copy.437.vec_ref, bf16[512,3072]{1,0:T(8,128)(2,1)} %get-tuple-element.74.slope_ref, ...), custom_call_target="tpu_custom_call" | custom-call | flops 4831838208 | bytes 21233664 | tf_op jit(solution)/shard_map/pallas_call | solution.py:379
  330.2 20.9 %shard_map.2430 = (f32[512,768]{1,0:T(8,128)}, bf16[512,768]{1,0:T(8,128)(2,1)}, bf16[512,768]{1,0:T(8,128)(2,1)}, bf16[2304,1536]{1,0:T(8,128)(2,1)}, f32[2,8,768]{2,1,0:T(8,128)}) custom-call(f32[512,768]{1,0:T(8,128)} %get-tuple-element.70.x_ref, f32[512,768]{1,0:T(8,128)} %get-tuple-element.75.dy_ref, f32[8,768]{1,0:T(8,128)} %copy.443.vec_ref, ...), custom_call_target="tpu_custom_call" | custom-call | flops 8455716864 | bytes 32243712 | tf_op jit(solution)/shard_map/pallas_call | solution.py:435
  351.2 8.5 %convolution_convert_fusion.7 = bf16[2304,384]{1,0:T(8,128)(2,1)} fusion(bf16[2304,1536]{1,0:T(8,128)(2,1)} %get-tuple-element.88, bf16[768,3200]{1,0:T(8,128)(2,1)} %bitcast.98.w_ref), kind=kOutput, calls=%fused_computation.31 | convolution fusion | flops 2718793728 | bytes 10027008 | tf_op jit(solution)/shard_map/dot_general | solution.py:36
  359.7 7.1 fusion.17
  366.8 16.2 %shard_map.2431 = (f32[512,768]{1,0:T(8,128)}, bf16[512,768]{1,0:T(8,128)(2,1)}, bf16[512,2304]{1,0:T(8,128)(2,1)}, f32[2,8,768]{2,1,0:T(8,128)}) custom-call(bf16[512,768]{1,0:T(8,128)(2,1)} %copy-done.31, f32[512,768]{1,0:T(8,128)} %get-tuple-element.78.dy_ref, f32[8,768]{1,0:T(8,128)} %copy.435.vec_ref, bf16[512,2304]{1,0:T(8,128)(2,1)} %get-tuple-element.79.qkv_ref, ...), custom_call_target="tpu_custom_call" | custom-call | flops 3221225472 | bytes 16515072 | tf_op jit(solution)/shard_map/pallas_call | solution.py:341
  397.3 7.4 copy.466
  404.7 4.7 convolution_convert_fusion.2
  438.4 12.2 %shard_map.2432 = (f32[512,768]{1,0:T(8,128)}, bf16[512,768]{1,0:T(8,128)(2,1)}, bf16[512,3072]{1,0:T(8,128)(2,1)}, f32[2,8,768]{2,1,0:T(8,128)}) custom-call(f32[512,768]{1,0:T(8,128)} %get-tuple-element.65.x_ref, f32[512,768]{1,0:T(8,128)} %convert_add_fusion.7.dy_ref, f32[8,768]{1,0:T(8,128)} %copy.437.vec_ref, ...), custom_call_target="tpu_custom_call" | custom-call | flops 4831838208 | bytes 21233664 | tf_op jit(solution)/shard_map/pallas_call | solution.py:379
  450.6 16.3 %shard_map.2433 = (f32[512,768]{1,0:T(8,128)}, bf16[512,768]{1,0:T(8,128)(2,1)}, bf16[512,2304]{1,0:T(8,128)(2,1)}, f32[2,8,768]{2,1,0:T(8,128)}) custom-call(bf16[512,768]{1,0:T(8,128)(2,1)} %x_ref.3, f32[512,768]{1,0:T(8,128)} %get-tuple-element.84.dy_ref, f32[8,768]{1,0:T(8,128)} %copy.435.vec_ref, bf16[512,2304]{1,0:T(8,128)(2,1)} %get-tuple-element.85.qkv_ref, ...), custom_call_target="tpu_custom_call" | custom-call | flops 3221225472 | bytes 16515072 | tf_op jit(solution)/shard_map/pallas_call | solution.py:341
  470.6 4.0 convolution_convert_fusion.5
  479.6 3.1 convolution_convert_fusion.1
  492.5 6.9 convolution_select_fusion
  533.5 3.8 collective-permute-start.107
  539.8 3.5 collective-permute-start.91
  545.9 5.0 collective-permute-done.91
  551.7 3.7 collective-permute-start.75
  558.5 3.7 collective-permute-done.75
  563.7 3.8 collective-permute-start.92
  570.3 5.3 collective-permute-done.92
  575.5 3.8 collective-permute-start.76
  582.6 3.3 collective-permute-done.76
  586.7 3.9 collective-permute-start.109
  592.7 6.5 collective-permute-done.95
  604.2 3.7 collective-permute-done.77
  611.4 76.8 %collective-permute-done.122 = f32[24,3200]{1,0:T(8,128)S(1)} collective-permute-done((f32[24,3200]{1,0:T(8,128)S(1)}, f32[24,3200]{1,0:T(8,128)S(1)}, u32[]{:S(2)}, u32[]{:S(2)}) %collective-permute-start.122) | collective-permute-done | bytes 307232 | tf_op jit(solution)/shard_map/ppermute | solution.py:504
  688.2 3.6 collective-permute-start.96
  693.9 5.0 collective-permute-done.96
  698.9 3.4 collective-permute-start.80
  705.6 3.4 collective-permute-start.110
  709.0 3.1 collective-permute-start.97
  717.4 3.9 collective-permute-done.110
  724.1 3.0 collective-permute-start.81
  (551 shorter events, 302.6 us)
Async XLA Ops:
  5.8 52.0 %collective-permute-start.48 = (bf16[24,3200]{1,0:T(8,128)(2,1)}, bf16[24,3200]{1,0:T(8,128)(2,1)}, u32[]{:S(2)}, u32[]{:S(2)}) collective-permute-start(bf16[24,3200]{1,0:T(8,128)(2,1)} %fusion.73), channel_id=1, source_target_pairs={{1,16},{3,18},{5,20},{7,22},{9,24},{11,26},{13,28},{15,30}} | collective-permute-start | bytes 460808 | tf_op jit(solution)/shard_map/ppermute | solution.py:504
  7.1 51.7 %collective-permute-start.47 = (bf16[24,3200]{1,0:T(8,128)(2,1)}, bf16[24,3200]{1,0:T(8,128)(2,1)}, u32[]{:S(2)}, u32[]{:S(2)}) collective-permute-start(bf16[24,3200]{1,0:T(8,128)(2,1)} %fusion.73), channel_id=1, source_target_pairs={{0,16},{2,18},{4,20},{6,22},{8,24},{10,26},{12,28},{14,30},{16,17}... | collective-permute-start | bytes 460808 | tf_op jit(solution)/shard_map/ppermute | solution.py:504
  20.2 39.6 %collective-permute-start.3 = (bf16[48,3200]{1,0:T(8,128)(2,1)}, bf16[48,3200]{1,0:T(8,128)(2,1)}, u32[]{:S(2)}, u32[]{:S(2)}) collective-permute-start(bf16[48,3200]{1,0:T(8,128)(2,1)} %pad_maximum_fusion.1), channel_id=1, source_target_pairs={{0,2},{1,3},{4,0},{5,1},{8,4},{9,5},{12,8},{13,9},{14,12},{15,13},... | collective-permute-start | bytes 921608 | tf_op jit(solution)/shard_map/ppermute | solution.py:504
  21.7 39.6 %collective-permute-start.1 = (bf16[48,3200]{1,0:T(8,128)(2,1)}, bf16[48,3200]{1,0:T(8,128)(2,1)}, u32[]{:S(2)}, u32[]{:S(2)}) collective-permute-start(bf16[48,3200]{1,0:T(8,128)(2,1)} %pad_maximum_fusion.1), channel_id=1, source_target_pairs={{0,4},{1,5},{4,8},{5,9},{8,12},{9,13},{12,14},{13,15},{14,10},{15,... | collective-permute-start | bytes 921608 | tf_op jit(solution)/shard_map/ppermute | solution.py:504
  22.2 39.9 %collective-permute-start = (bf16[48,3200]{1,0:T(8,128)(2,1)}, bf16[48,3200]{1,0:T(8,128)(2,1)}, u32[]{:S(2)}, u32[]{:S(2)}) collective-permute-start(bf16[48,3200]{1,0:T(8,128)(2,1)} %pad_maximum_fusion.1), channel_id=1, source_target_pairs={{0,1},{1,0},{2,3},{3,2},{4,5},{5,4},{6,7},{7,6},{8,9},{9,8},{10,11... | collective-permute-start | bytes 921608 | tf_op jit(solution)/shard_map/ppermute | solution.py:504
  61.3 16.9 %collective-permute-start.4 = (bf16[48,3200]{1,0:T(8,128)(2,1)}, bf16[48,3200]{1,0:T(8,128)(2,1)S(1)}, u32[]{:S(2)}, u32[]{:S(2)}) collective-permute-start(bf16[48,3200]{1,0:T(8,128)(2,1)} %collective-permute-done.3), channel_id=1, source_target_pairs={{0,1},{1,0},{2,3},{3,2},{4,5},{5,4},{6,7},{7,6},{8,9},{9,8},{10,11... | collective-permute-start | bytes 921608 | tf_op jit(solution)/shard_map/ppermute | solution.py:504
  71.2 17.0 %collective-permute-start.18 = (bf16[48,3072]{1,0:T(8,128)(2,1)S(1)}, bf16[48,3072]{1,0:T(8,128)(2,1)S(1)}, u32[]{:S(2)}, u32[]{:S(2)}) collective-permute-start(bf16[48,3072]{1,0:T(8,128)(2,1)S(1)} %copy-done.12), channel_id=1, source_target_pairs={{0,2},{1,3},{4,0},{5,1},{8,4},{9,5},{12,8},{13,9},{14,12},{15,13},... | collective-permute-start | bytes 884744 | tf_op jit(solution)/shard_map/ppermute | solution.py:504
  76.5 21.2 %collective-permute-start.52 = (bf16[48,3200]{1,0:T(8,128)(2,1)S(1)}, bf16[48,3200]{1,0:T(8,128)(2,1)S(1)}, u32[]{:S(2)}, u32[]{:S(2)}) collective-permute-start(bf16[48,3200]{1,0:T(8,128)(2,1)S(1)} %pad_maximum_fusion.2), channel_id=1, source_target_pairs={{16,18},{17,19},{20,16},{21,17},{24,20},{25,21},{28,24},{29,25},{3... | collective-permute-start | bytes 921608 | tf_op jit(solution)/shard_map/ppermute | solution.py:504
  83.9 32.2 %collective-permute-start.11 = (bf16[48,3200]{1,0:T(8,128)(2,1)S(1)}, bf16[48,3200]{1,0:T(8,128)(2,1)S(1)}, u32[]{:S(2)}, u32[]{:S(2)}) collective-permute-start(bf16[48,3200]{1,0:T(8,128)(2,1)S(1)} %collective-permute-done.7), channel_id=1, source_target_pairs={{0,2},{1,3},{4,0},{5,1},{8,4},{9,5},{12,8},{13,9},{14,12},{15,13},... | collective-permute-start | bytes 921608 | tf_op jit(solution)/shard_map/ppermute | solution.py:504
  88.8 19.8 %collective-permute-start.22 = (bf16[48,3072]{1,0:T(8,128)(2,1)S(1)}, bf16[48,3072]{1,0:T(8,128)(2,1)S(1)}, u32[]{:S(2)}, u32[]{:S(2)}) collective-permute-start(bf16[48,3072]{1,0:T(8,128)(2,1)S(1)} %collective-permute-done.18), channel_id=1, source_target_pairs={{0,2},{1,3},{4,0},{5,1},{8,4},{9,5},{12,8},{13,9},{14,12},{15,13},... | collective-permute-start | bytes 884744 | tf_op jit(solution)/shard_map/ppermute | solution.py:504
  99.2 40.1 %collective-permute-start.56 = (bf16[48,3200]{1,0:T(8,128)(2,1)S(1)}, bf16[48,3200]{1,0:T(8,128)(2,1)}, u32[]{:S(2)}, u32[]{:S(2)}) collective-permute-start(bf16[48,3200]{1,0:T(8,128)(2,1)S(1)} %collective-permute-done.52), channel_id=1, source_target_pairs={{16,18},{17,19},{20,16},{21,17},{24,20},{25,21},{28,24},{29,25},{3... | collective-permute-start | bytes 921608 | tf_op jit(solution)/shard_map/ppermute | solution.py:504
  117.4 48.1 %collective-permute-start.33 = (bf16[192,768]{1,0:T(8,128)(2,1)}, bf16[192,768]{1,0:T(8,128)(2,1)}, u32[]{:S(2)}, u32[]{:S(2)}) collective-permute-start(bf16[192,768]{1,0:T(8,128)(2,1)} %convert_bitcast_fusion), channel_id=1, source_target_pairs={{0,2},{1,3},{4,0},{5,1},{8,4},{9,5},{12,8},{13,9},{14,12},{15,13},... | collective-permute-start | bytes 884744 | tf_op jit(solution)/shard_map/ppermute | solution.py:504
  120.7 21.5 %collective-permute-start.31 = (bf16[192,768]{1,0:T(8,128)(2,1)}, bf16[192,768]{1,0:T(8,128)(2,1)S(1)}, u32[]{:S(2)}, u32[]{:S(2)}) collective-permute-start(bf16[192,768]{1,0:T(8,128)(2,1)} %convert_bitcast_fusion), channel_id=1, source_target_pairs={{0,4},{1,5},{4,8},{5,9},{8,12},{9,13},{12,14},{13,15},{14,10},{15,... | collective-permute-start | bytes 884744 | tf_op jit(solution)/shard_map/ppermute | solution.py:504
  121.2 18.8 %collective-permute-start.30 = (bf16[192,768]{1,0:T(8,128)(2,1)}, bf16[192,768]{1,0:T(8,128)(2,1)S(1)}, u32[]{:S(2)}, u32[]{:S(2)}) collective-permute-start(bf16[192,768]{1,0:T(8,128)(2,1)} %convert_bitcast_fusion), channel_id=1, source_target_pairs={{0,1},{1,0},{2,3},{3,2},{4,5},{5,4},{6,7},{7,6},{8,9},{9,8},{10,11... | collective-permute-start | bytes 884744 | tf_op jit(solution)/shard_map/ppermute | solution.py:504
  140.1 40.0 %collective-permute-start.60 = (bf16[48,3200]{1,0:T(8,128)(2,1)}, bf16[48,3200]{1,0:T(8,128)(2,1)}, u32[]{:S(2)}, u32[]{:S(2)}) collective-permute-start(bf16[48,3200]{1,0:T(8,128)(2,1)} %collective-permute-done.56), channel_id=1, source_target_pairs={{16,18},{17,19},{20,16},{21,17},{24,20},{25,21},{28,24},{29,25},{3... | collective-permute-start | bytes 921608 | tf_op jit(solution)/shard_map/ppermute | solution.py:504
  146.1 19.8 %collective-permute-start.58 = (bf16[48,3200]{1,0:T(8,128)(2,1)}, bf16[48,3200]{1,0:T(8,128)(2,1)}, u32[]{:S(2)}, u32[]{:S(2)}) collective-permute-start(bf16[48,3200]{1,0:T(8,128)(2,1)} %collective-permute-done.54), channel_id=1, source_target_pairs={{16,20},{17,21},{20,24},{21,25},{24,28},{25,29},{28,30},{29,31},{3... | collective-permute-start | bytes 921608 | tf_op jit(solution)/shard_map/ppermute | solution.py:504
  147.5 32.8 %collective-permute-start.28 = (bf16[48,3072]{1,0:T(8,128)(2,1)}, bf16[48,3072]{1,0:T(8,128)(2,1)}, u32[]{:S(2)}, u32[]{:S(2)}) collective-permute-start(bf16[48,3072]{1,0:T(8,128)(2,1)} %collective-permute-done.26), channel_id=1, source_target_pairs={{0,2},{1,3},{4,0},{5,1},{8,4},{9,5},{12,8},{13,9},{14,12},{15,13},... | collective-permute-start | bytes 884744 | tf_op jit(solution)/shard_map/ppermute | solution.py:504
  152.1 24.8 %collective-permute-start.27 = (bf16[48,3072]{1,0:T(8,128)(2,1)}, bf16[48,3072]{1,0:T(8,128)(2,1)}, u32[]{:S(2)}, u32[]{:S(2)}) collective-permute-start(bf16[48,3072]{1,0:T(8,128)(2,1)} %collective-permute-done.26), channel_id=1, source_target_pairs={{0,1},{1,0},{2,3},{3,2},{4,5},{5,4},{6,7},{7,6},{8,9},{9,8},{10,11... | collective-permute-start | bytes 884744 | tf_op jit(solution)/shard_map/ppermute | solution.py:504
  165.9 21.3 %collective-permute-start.37 = (bf16[192,768]{1,0:T(8,128)(2,1)}, bf16[192,768]{1,0:T(8,128)(2,1)}, u32[]{:S(2)}, u32[]{:S(2)}) collective-permute-start(bf16[192,768]{1,0:T(8,128)(2,1)} %collective-permute-done.33), channel_id=1, source_target_pairs={{0,2},{1,3},{4,0},{5,1},{8,4},{9,5},{12,8},{13,9},{14,12},{15,13},... | collective-permute-start | bytes 884744 | tf_op jit(solution)/shard_map/ppermute | solution.py:504
  187.5 15.5 %collective-permute-start.41 = (bf16[192,768]{1,0:T(8,128)(2,1)}, bf16[192,768]{1,0:T(8,128)(2,1)}, u32[]{:S(2)}, u32[]{:S(2)}) collective-permute-start(bf16[192,768]{1,0:T(8,128)(2,1)} %collective-permute-done.37), channel_id=1, source_target_pairs={{0,2},{1,3},{4,0},{5,1},{8,4},{9,5},{12,8},{13,9},{14,12},{15,13},... | collective-permute-start | bytes 884744 | tf_op jit(solution)/shard_map/ppermute | solution.py:504
  188.9 17.0 %collective-permute-start.38 = (bf16[192,768]{1,0:T(8,128)(2,1)}, bf16[192,768]{1,0:T(8,128)(2,1)S(1)}, u32[]{:S(2)}, u32[]{:S(2)}) collective-permute-start(bf16[192,768]{1,0:T(8,128)(2,1)} %collective-permute-done.37), channel_id=1, source_target_pairs={{0,1},{1,0},{2,3},{3,2},{4,5},{5,4},{6,7},{7,6},{8,9},{9,8},{10,11... | collective-permute-start | bytes 884744 | tf_op jit(solution)/shard_map/ppermute | solution.py:504
  200.9 21.0 %collective-permute-start.43 = (bf16[192,768]{1,0:T(8,128)(2,1)}, bf16[192,768]{1,0:T(8,128)(2,1)}, u32[]{:S(2)}, u32[]{:S(2)}) collective-permute-start(bf16[192,768]{1,0:T(8,128)(2,1)} %collective-permute-done.39), channel_id=1, source_target_pairs={{0,4},{1,5},{4,8},{5,9},{8,12},{9,13},{12,14},{13,15},{14,10},{15,... | collective-permute-start | bytes 884744 | tf_op jit(solution)/shard_map/ppermute | solution.py:504
  203.0 19.0 %collective-permute-start.40 = (bf16[192,768]{1,0:T(8,128)(2,1)}, bf16[192,768]{1,0:T(8,128)(2,1)}, u32[]{:S(2)}, u32[]{:S(2)}) collective-permute-start(bf16[192,768]{1,0:T(8,128)(2,1)} %collective-permute-done.39), channel_id=1, source_target_pairs={{0,1},{1,0},{2,3},{3,2},{4,5},{5,4},{6,7},{7,6},{8,9},{9,8},{10,11... | collective-permute-start | bytes 884744 | tf_op jit(solution)/shard_map/ppermute | solution.py:504
  203.0 22.4 %collective-permute-start.42 = (bf16[192,768]{1,0:T(8,128)(2,1)}, bf16[192,768]{1,0:T(8,128)(2,1)}, u32[]{:S(2)}, u32[]{:S(2)}) collective-permute-start(bf16[192,768]{1,0:T(8,128)(2,1)} %collective-permute-done.41), channel_id=1, source_target_pairs={{0,1},{1,0},{2,3},{3,2},{4,5},{5,4},{6,7},{7,6},{8,9},{9,8},{10,11... | collective-permute-start | bytes 884744 | tf_op jit(solution)/shard_map/ppermute | solution.py:504
  238.3 41.9 %collective-permute-start.46 = (bf16[256,768]{1,0:T(8,128)(2,1)}, bf16[256,768]{1,0:T(8,128)(2,1)S(1)}, u32[]{:S(2)}, u32[]{:S(2)}) collective-permute-start(bf16[256,768]{1,0:T(8,128)(2,1)} %get-tuple-element.69), channel_id=1, source_target_pairs={{0,16},{1,17},{2,18},{3,19},{4,20},{5,21},{6,22},{7,23},{8,24},{9,... | collective-permute-start | bytes 1179656 | tf_op jit(solution)/shard_map/ppermute | solution.py:675
  387.1 46.5 %collective-permute-start.64 = (bf16[512,768]{1,0:T(8,128)(2,1)}, bf16[512,768]{1,0:T(8,128)(2,1)}, u32[]{:S(2)}, u32[]{:S(2)}) collective-permute-start(bf16[512,768]{1,0:T(8,128)(2,1)} %convert_element_type.698), channel_id=1, source_target_pairs={{16,0},{17,1},{18,2},{19,3},{20,4},{21,5},{22,6},{23,7},{24,8},{25... | collective-permute-start | bytes 2359304 | tf_op jit(solution)/shard_map/ppermute | solution.py:686
  388.4 101.7 %collective-permute-start.65 = (bf16[2304,384]{1,0:T(8,128)(2,1)}, bf16[2304,384]{1,0:T(8,128)(2,1)}, u32[]{:S(2)}, u32[]{:S(2)}) collective-permute-start(bf16[2304,384]{1,0:T(8,128)(2,1)} %convolution_convert_fusion.7), channel_id=1, source_target_pairs={{16,0},{17,1},{18,2},{19,3},{20,4},{21,5},{22,6},{23,7},{24,8},{25... | collective-permute-start | bytes 5308424 | tf_op jit(solution)/shard_map/ppermute | solution.py:709
  411.1 88.3 %collective-permute-start.98 = (bf16[8,192,768]{2,1,0:T(8,128)(2,1)}, bf16[8,192,768]{2,1,0:T(8,128)(2,1)}, u32[]{:S(2)}, u32[]{:S(2)}) collective-permute-start(bf16[8,192,768]{2,1,0:T(8,128)(2,1)} %dynamic-slice_bitcast_fusion.4), channel_id=1, source_target_pairs={{16,17},{17,16},{18,19},{19,18},{20,21},{21,20},{22,23},{23,22},{2... | collective-permute-start | bytes 7077896 | tf_op jit(solution)/shard_map/ppermute | solution.py:504
  422.4 85.5 %collective-permute-start.66 = (bf16[8,48,3200]{2,1,0:T(8,128)(2,1)}, bf16[8,48,3200]{2,1,0:T(8,128)(2,1)}, u32[]{:S(2)}, u32[]{:S(2)}) collective-permute-start(bf16[8,48,3200]{2,1,0:T(8,128)(2,1)} %dynamic-slice_bitcast_fusion.2), channel_id=1, source_target_pairs={{16,17},{17,16},{18,19},{19,18},{20,21},{21,20},{22,23},{23,22},{2... | collective-permute-start | bytes 7372808 | tf_op jit(solution)/shard_map/ppermute | solution.py:504
  424.5 87.0 %collective-permute-start.114 = (bf16[8,48,3200]{2,1,0:T(8,128)(2,1)}, bf16[8,48,3200]{2,1,0:T(8,128)(2,1)}, u32[]{:S(2)}, u32[]{:S(2)}) collective-permute-start(bf16[8,48,3200]{2,1,0:T(8,128)(2,1)} %dynamic-slice_bitcast_fusion), channel_id=1, source_target_pairs={{16,17},{17,16},{18,19},{19,18},{20,21},{21,20},{22,23},{23,22},{2... | collective-permute-start | bytes 7372808 | tf_op jit(solution)/shard_map/ppermute | solution.py:504
  433.6 70.3 %collective-permute-start.82 = (bf16[8,48,3072]{2,1,0:T(8,128)(2,1)}, bf16[8,48,3072]{2,1,0:T(8,128)(2,1)}, u32[]{:S(2)}, u32[]{:S(2)}) collective-permute-start(bf16[8,48,3072]{2,1,0:T(8,128)(2,1)} %dynamic-slice_bitcast_fusion.6), channel_id=1, source_target_pairs={{16,17},{17,16},{18,19},{19,18},{20,21},{21,20},{22,23},{23,22},{2... | collective-permute-start | bytes 7077896 | tf_op jit(solution)/shard_map/ppermute | solution.py:504
  490.1 34.0 %collective-permute-start.106 = (bf16[8,192,768]{2,1,0:T(8,128)(2,1)}, bf16[8,192,768]{2,1,0:T(8,128)(2,1)}, u32[]{:S(2)}, u32[]{:S(2)}) collective-permute-start(bf16[8,192,768]{2,1,0:T(8,128)(2,1)} %dynamic-slice_bitcast_fusion.3), channel_id=1, source_target_pairs={{0,1},{1,0},{2,3},{3,2},{4,5},{5,4},{6,7},{7,6},{8,9},{9,8},{10,11... | collective-permute-start | bytes 7077896 | tf_op jit(solution)/shard_map/ppermute | solution.py:504
  499.4 29.5 %collective-permute-start.74 = (bf16[8,48,3200]{2,1,0:T(8,128)(2,1)}, bf16[8,48,3200]{2,1,0:T(8,128)(2,1)}, u32[]{:S(2)}, u32[]{:S(2)}) collective-permute-start(bf16[8,48,3200]{2,1,0:T(8,128)(2,1)} %dynamic-slice_bitcast_fusion.1), channel_id=1, source_target_pairs={{0,1},{1,0},{2,3},{3,2},{4,5},{5,4},{6,7},{7,6},{8,9},{9,8},{10,11... | collective-permute-start | bytes 7372808 | tf_op jit(solution)/shard_map/ppermute | solution.py:504
  527.2 176.0 %collective-permute-start.85 = (bf16[48,3072]{1,0:T(8,128)(2,1)S(1)}, bf16[48,3072]{1,0:T(8,128)(2,1)S(1)}, u32[]{:S(2)}, u32[]{:S(2)}) collective-permute-start(bf16[48,3072]{1,0:T(8,128)(2,1)S(1)} %get-tuple-element.152), channel_id=1, source_target_pairs={{16,20},{17,21},{20,24},{21,25},{24,28},{25,29},{28,30},{29,31},{3... | collective-permute-start | bytes 884744 | tf_op jit(solution)/shard_map/ppermute | solution.py:504
  533.5 18.2 %collective-permute-start.107 = (bf16[192,768]{1,0:T(8,128)(2,1)S(1)}, bf16[192,768]{1,0:T(8,128)(2,1)S(1)}, u32[]{:S(2)}, u32[]{:S(2)}) collective-permute-start(bf16[192,768]{1,0:T(8,128)(2,1)S(1)} %get-tuple-element.150), channel_id=1, source_target_pairs={{0,4},{1,5},{4,8},{5,9},{8,12},{9,13},{12,14},{13,15},{14,10},{15,... | collective-permute-start | bytes 884744 | tf_op jit(solution)/shard_map/ppermute | solution.py:504
  537.4 64.5 %collective-permute-start.111 = (bf16[192,768]{1,0:T(8,128)(2,1)S(1)}, bf16[192,768]{1,0:T(8,128)(2,1)S(1)}, u32[]{:S(2)}, u32[]{:S(2)}) collective-permute-start(bf16[192,768]{1,0:T(8,128)(2,1)S(1)} %get-tuple-element.151), channel_id=1, source_target_pairs={{0,2},{1,3},{4,0},{5,1},{8,4},{9,5},{12,8},{13,9},{14,12},{15,13},... | collective-permute-start | bytes 884744 | tf_op jit(solution)/shard_map/ppermute | solution.py:504
  543.5 24.1 %collective-permute-start.94 = (bf16[48,3072]{1,0:T(8,128)(2,1)S(1)}, bf16[48,3072]{1,0:T(8,128)(2,1)S(1)}, u32[]{:S(2)}, u32[]{:S(2)}) collective-permute-start(bf16[48,3072]{1,0:T(8,128)(2,1)S(1)} %get-tuple-element.159), channel_id=1, source_target_pairs={{0,2},{1,3},{4,0},{5,1},{8,4},{9,5},{12,8},{13,9},{14,12},{15,13},... | collective-permute-start | bytes 884744 | tf_op jit(solution)/shard_map/ppermute | solution.py:504
  556.2 47.3 %collective-permute-start.79 = (bf16[48,3200]{1,0:T(8,128)(2,1)S(1)}, bf16[48,3200]{1,0:T(8,128)(2,1)S(1)}, u32[]{:S(2)}, u32[]{:S(2)}) collective-permute-start(bf16[48,3200]{1,0:T(8,128)(2,1)S(1)} %get-tuple-element.143), channel_id=1, source_target_pairs={{0,2},{1,3},{4,0},{5,1},{8,4},{9,5},{12,8},{13,9},{14,12},{15,13},... | collective-permute-start | bytes 921608 | tf_op jit(solution)/shard_map/ppermute | solution.py:504
  586.7 16.0 %collective-permute-start.109 = (bf16[192,768]{1,0:T(8,128)(2,1)S(1)}, bf16[192,768]{1,0:T(8,128)(2,1)S(1)}, u32[]{:S(2)}, u32[]{:S(2)}) collective-permute-start(bf16[192,768]{1,0:T(8,128)(2,1)S(1)} %fusion.47), channel_id=1, source_target_pairs={{0,4},{1,5},{4,8},{5,9},{8,12},{9,13},{12,14},{13,15},{14,10},{15,... | collective-permute-start | bytes 884744 | tf_op jit(solution)/shard_map/ppermute | solution.py:504
  602.0 103.6 %collective-permute-start.102 = (bf16[192,768]{1,0:T(8,128)(2,1)S(1)}, bf16[192,768]{1,0:T(8,128)(2,1)S(1)}, u32[]{:S(2)}, u32[]{:S(2)}) collective-permute-start(bf16[192,768]{1,0:T(8,128)(2,1)S(1)} %get-tuple-element.144), channel_id=1, source_target_pairs={{16,20},{17,21},{20,24},{21,25},{24,28},{25,29},{28,30},{29,31},{3... | collective-permute-start | bytes 884744 | tf_op jit(solution)/shard_map/ppermute | solution.py:504
  602.7 109.5 %collective-permute-start.105 = (bf16[192,768]{1,0:T(8,128)(2,1)S(1)}, bf16[192,768]{1,0:T(8,128)(2,1)S(1)}, u32[]{:S(2)}, u32[]{:S(2)}) collective-permute-start(bf16[192,768]{1,0:T(8,128)(2,1)S(1)} %fusion.53), channel_id=1, source_target_pairs={{16,18},{17,19},{20,16},{21,17},{24,20},{25,21},{28,24},{29,25},{3... | collective-permute-start | bytes 884744 | tf_op jit(solution)/shard_map/ppermute | solution.py:504
  608.0 80.2 %collective-permute-start.122 = (f32[24,3200]{1,0:T(8,128)S(1)}, f32[24,3200]{1,0:T(8,128)S(1)}, u32[]{:S(2)}, u32[]{:S(2)}) collective-permute-start(f32[24,3200]{1,0:T(8,128)S(1)} %get-tuple-element.163), channel_id=1, source_target_pairs={{16,0},{18,2},{20,4},{22,6},{24,8},{26,10},{28,12},{30,14},{17,16}... | collective-permute-start | bytes 921608 | tf_op jit(solution)/shard_map/ppermute | solution.py:504
  609.4 92.9 %collective-permute-start.112 = (bf16[192,768]{1,0:T(8,128)(2,1)S(1)}, bf16[192,768]{1,0:T(8,128)(2,1)S(1)}, u32[]{:S(2)}, u32[]{:S(2)}) collective-permute-start(bf16[192,768]{1,0:T(8,128)(2,1)S(1)} %get-tuple-element.149), channel_id=1, source_target_pairs={{0,2},{1,3},{4,0},{5,1},{8,4},{9,5},{12,8},{13,9},{14,12},{15,13},... | collective-permute-start | bytes 884744 | tf_op jit(solution)/shard_map/ppermute | solution.py:504
  705.6 15.7 %collective-permute-start.110 = (bf16[192,768]{1,0:T(8,128)(2,1)S(1)}, bf16[192,768]{1,0:T(8,128)(2,1)S(1)}, u32[]{:S(2)}, u32[]{:S(2)}) collective-permute-start(bf16[192,768]{1,0:T(8,128)(2,1)S(1)} %get-tuple-element.148), channel_id=1, source_target_pairs={{0,4},{1,5},{4,8},{5,9},{8,12},{9,13},{12,14},{13,15},{14,10},{15,... | collective-permute-start | bytes 884744 | tf_op jit(solution)/shard_map/ppermute | solution.py:504
  709.0 15.0 %collective-permute-start.97 = (bf16[48,3072]{1,0:T(8,128)(2,1)S(1)}, bf16[48,3072]{1,0:T(8,128)(2,1)S(1)}, u32[]{:S(2)}, u32[]{:S(2)}) collective-permute-start(bf16[48,3072]{1,0:T(8,128)(2,1)S(1)} %fusion.60), channel_id=1, source_target_pairs={{0,2},{1,3},{4,0},{5,1},{8,4},{9,5},{12,8},{13,9},{14,12},{15,13},... | collective-permute-start | bytes 884744 | tf_op jit(solution)/shard_map/ppermute | solution.py:504
  712.2 19.3 %collective-permute-start.69 = (bf16[48,3200]{1,0:T(8,128)(2,1)S(1)}, bf16[48,3200]{1,0:T(8,128)(2,1)S(1)}, u32[]{:S(2)}, u32[]{:S(2)}) collective-permute-start(bf16[48,3200]{1,0:T(8,128)(2,1)S(1)} %get-tuple-element.136), channel_id=1, source_target_pairs={{16,20},{17,21},{20,24},{21,25},{24,28},{25,29},{28,30},{29,31},{3... | collective-permute-start | bytes 921608 | tf_op jit(solution)/shard_map/ppermute | solution.py:504
  712.9 18.6 %collective-permute-start.73 = (bf16[48,3200]{1,0:T(8,128)(2,1)S(1)}, bf16[48,3200]{1,0:T(8,128)(2,1)S(1)}, u32[]{:S(2)}, u32[]{:S(2)}) collective-permute-start(bf16[48,3200]{1,0:T(8,128)(2,1)S(1)} %fusion.40), channel_id=1, source_target_pairs={{16,18},{17,19},{20,16},{21,17},{24,20},{25,21},{28,24},{29,25},{3... | collective-permute-start | bytes 921608 | tf_op jit(solution)/shard_map/ppermute | solution.py:504
  715.0 16.5 %collective-permute-start.78 = (bf16[48,3200]{1,0:T(8,128)(2,1)S(1)}, bf16[48,3200]{1,0:T(8,128)(2,1)S(1)}, u32[]{:S(2)}, u32[]{:S(2)}) collective-permute-start(bf16[48,3200]{1,0:T(8,128)(2,1)S(1)} %get-tuple-element.140), channel_id=1, source_target_pairs={{0,4},{1,5},{4,8},{5,9},{8,12},{9,13},{12,14},{13,15},{14,10},{15,... | collective-permute-start | bytes 921608 | tf_op jit(solution)/shard_map/ppermute | solution.py:504
  (137 other events, 1175.2 us)
